TPU v7x, 512 devices: a whole 4x8x8 slice. The times are simulated.
512 devices in a mesh: prow: 16 (over z, core), pcol: 32 (over y, x).
Axes of the slice: x: 4, y: 8, z: 8, core: 2. Of those that a mesh axis runs over, the one named last changes fastest.
Arguments:
- covariance: float32 [2, 16, 512, 1, 32, 512], P(None, 'prow', None, None, 'pcol'), may hold values from 0 to 5, as said below
- observations: float32 [2, 16, 512, 256], P(None, 'prow', 'pcol'), may hold values from -6 to 6
Outputs:
- factor: float32 [2, 16, 512, 1, 32, 512], P(None, 'prow', None, None, 'pcol')
- reduced: float32 [2, 16, 512, 256], P(None, 'prow', 'pcol')
Inputs may be any that keep to these rules, and one draw needn't show every extreme that they name: Symmetric positive definite: a Matern covariance of smoothness 3/2 and range 0.1 between random points in the unit square, with a positive scale on each point and a positive nugget added on the diagonal.
All inputs are finite; a program needn't handle non-finite values.
Results may differ from a plain program's by a relative error of at most 0.0003.
Values sent between devices are 32-bit elements; how exact they have to be, the bound alone decides.
A program may use at most 64 MiB of HBM per device.

v0:
```python
import jax
import jax.numpy as jnp
from jax import lax
from jax.sharding import PartitionSpec as P

precision_mode = lax.Precision.HIGHEST


def broadcast(block, axis, holder):
    block = jnp.where(lax.axis_index(axis) == holder, block, jnp.zeros_like(block))
    return lax.psum(block, axis)


def times_inverse(stacked_tiles, inverse):
    return jnp.einsum(
        "sab,cb->sac",
        stacked_tiles,
        inverse,
        precision=precision_mode,
        preferred_element_type=jnp.float32,
    )


def settle(column_factor, diag_rows, row_tile, current):
    column_factor = jnp.where((row_tile < current)[:, None, None], 0.0, column_factor)
    return jnp.where((row_tile == current)[:, None, None], diag_rows[None], column_factor)


def body(covariance, observations):
    rows_here = covariance.shape[0]
    tile_size = covariance.shape[2]
    cols_here = covariance.shape[3]
    sub_rows = observations.shape[2]
    rhs_width = observations.shape[3]
    row_count = lax.axis_size("prow")
    col_count = lax.axis_size("pcol")
    row_pos = lax.axis_index("prow")
    col_pos = lax.axis_index("pcol")
    cross_count = tile_size // row_count
    identity = jnp.eye(tile_size, dtype=jnp.float32)
    blocks = covariance.reshape(rows_here, tile_size, cols_here, tile_size)
    right_rows = observations.reshape(rows_here, sub_rows, rhs_width)
    row_tile = jnp.arange(rows_here, dtype=jnp.int32) * row_count + row_pos
    col_tile = jnp.arange(cols_here, dtype=jnp.int32) * col_count + col_pos
    for current in range(2):
        root_row = current % row_count
        root_col = current % col_count
        local_row = current // row_count
        local_col = current // col_count
        diagonal = broadcast(blocks[local_row, :, local_col, :], "prow", root_row)
        diag_factor = jnp.linalg.cholesky(diagonal)
        inverse = jax.scipy.linalg.solve_triangular(diag_factor, identity, lower=True)
        whole_panel = settle(
            times_inverse(blocks[:, :, local_col, :], inverse), diag_factor, row_tile, current
        )
        received = lax.all_to_all(whole_panel, "pcol", split_axis=1, concat_axis=0, tiled=True)
        own_share = lax.slice_in_dim(
            received, root_col * rows_here, (root_col + 1) * rows_here, axis=0
        )
        column_factor = lax.all_gather(own_share, "pcol", axis=1, tiled=True)
        crossed = []
        target = 0 + col_pos
        portion = lax.dynamic_index_in_dim(column_factor, target // row_count, 0, keepdims=False)
        spread = lax.all_to_all(portion, "prow", split_axis=0, concat_axis=0, tiled=True)
        mine = lax.dynamic_slice_in_dim(spread, target % row_count * cross_count, cross_count, 0)
        crossed.append(lax.all_gather(mine, "prow", axis=0, tiled=True))
        crossed = jnp.stack(crossed)
        product = jnp.einsum(
            "sab,tcb->satc",
            column_factor,
            crossed,
            precision=precision_mode,
            preferred_element_type=jnp.float32,
        )
        update_mask = (row_tile[:, None] >= col_tile[None, :]) & (col_tile[None, :] > current)
        blocks = jnp.where(
            (col_tile == current)[None, None, :, None],
            column_factor[:, :, None, :],
            jnp.where(update_mask[:, None, :, None], blocks - product, blocks),
        )
        pieces = right_rows[local_row]
        gathered = lax.all_gather(pieces, "pcol", axis=0, tiled=True)
        solved = jax.scipy.linalg.solve_triangular(column_factor[local_row], gathered, lower=True)
        solved = broadcast(solved, "prow", root_row)
        own_rows = lax.dynamic_slice_in_dim(solved, col_pos * sub_rows, sub_rows, 0)
        strips = lax.dynamic_slice_in_dim(column_factor, col_pos * sub_rows, sub_rows, 1)
        change = jnp.einsum(
            "sab,bc->sac",
            strips,
            solved,
            precision=precision_mode,
            preferred_element_type=jnp.float32,
        )
        right_rows = jnp.where(
            (row_tile == current)[:, None, None],
            own_rows[None],
            jnp.where((row_tile > current)[:, None, None], right_rows - change, right_rows),
        )
    keeping = row_tile[:, None] >= col_tile[None, :]
    blocks = jnp.where(keeping[:, None, :, None], blocks, 0.0)
    return (blocks.reshape(covariance.shape), right_rows.reshape(observations.shape))


def solution(mesh):
    return jax.shard_map(
        body,
        mesh=mesh,
        in_specs=(P(None, "prow", None, None, "pcol", None), P(None, "prow", "pcol", None)),
        out_specs=(P(None, "prow", None, None, "pcol", None), P(None, "prow", "pcol", None)),
        check_vma=False,
    )
```

profile of v0, /device:TPU:1, one launch (start us, length us, event | category | flops | bytes accessed | tf_op | source)
XLA Modules:
  0.0 1265.0 jit_solution(12915858958863171359)
XLA Ops:
  11.7 4.4 copy.82
  16.2 117.7 %all-reduce.6.cloned.1.call-done = f32[512,512]{0,1:T(8,128)} async-done(((f32[512,512]{0,1:T(8,128)}), f32[512,512]{0,1:T(8,128)}) %all-reduce.6.cloned.1.call-update) | async-done | bytes 1048592 | tf_op jit(solution)/shard_map/psum | solution.py:11
  134.0 2.6 copy.48
  139.3 11.7 cholesky.286
  151.0 9.8 custom-call.31
  165.1 11.7 cholesky.305
  177.5 10.1 custom-call.32
  190.0 11.7 cholesky.326
  203.1 9.8 custom-call.33
  215.1 11.7 cholesky.343
  231.7 2.8 fusion.39
  234.5 11.2 while.8
  235.2 2.2 bitcast_dynamic-update-slice_fusion.8
  238.0 2.2 bitcast_dynamic-update-slice_fusion.8
  240.8 2.2 bitcast_dynamic-update-slice_fusion.8
  243.6 2.1 bitcast_dynamic-update-slice_fusion.8
  245.7 39.9 %custom-call.34 = f32[4,128,128]{1,2,0:T(8,128)} custom-call(f32[4,128,128]{2,1,0:T(8,128)S(1)} %get-tuple-element.33), custom_call_target="InvertDiagBlocksLowerTriangular" | custom-call | tf_op jit(solution)/shard_map/jit(_solve_triangular)/triangular_solve | solution.py:52
  294.2 2.5 copy.49
  296.7 7.0 bitcast_select_fusion
  303.7 4.1 copy.52
  307.8 56.5 %all_to_all.54 = f32[2,512,512]{2,0,1:T(2,128)S(1)} all-to-all(f32[2,512,512]{2,0,1:T(2,128)} %copy.52), channel_id=1, replica_groups=mesh['prow'=16,'pcol'=32] {'pcol'}, dimensions={1} | all-to-all | bytes 4194304 | tf_op jit(solution)/shard_map/all_to_all | solution.py:56
  365.5 76.6 %all-gather.13.cloned.1.call-done = f32[1,2,512,512]{3,1,0,2:T(2,128)} async-done(((f32[1,2,16,512]{3,1,0,2:T(2,128)}), f32[1,2,512,512]{3,1,0,2:T(2,128)}) %all-gather.13.cloned.1.call-update) | async-done | bytes 2097168 | tf_op jit(solution)/shard_map/all_gather | solution.py:60
  442.1 5.0 fusion.154
  448.2 11.8 all-to-all-start.1
  460.1 4.6 copy.50
  464.7 41.6 %all-gather.2 = f32[1,1,512,256]{3,2,1,0:T(8,128)} all-gather(f32[1,1,16,256]{3,2,1,0:T(8,128)S(1)} %slice-done.1), channel_id=4, replica_groups=mesh['prow'=16,'pcol'=32] {'pcol'}, dimensions={2}, use_global_device_ids=true | all-gather | bytes 540672 | tf_op jit(solution)/shard_map/all_gather | solution.py:82
  506.4 2.4 bitcast_select_fusion.1
  510.3 11.6 while.10
  511.0 2.3 bitcast_dynamic-update-slice_fusion.10
  513.9 2.3 bitcast_dynamic-update-slice_fusion.10
  516.8 2.3 bitcast_dynamic-update-slice_fusion.10
  519.7 2.2 bitcast_dynamic-update-slice_fusion.10
  522.7 40.1 %custom-call.39 = f32[4,128,128]{1,2,0:T(8,128)S(1)} custom-call(f32[4,128,128]{2,1,0:T(8,128)} %copy-done.12), custom_call_target="InvertDiagBlocksLowerTriangular" | custom-call | tf_op jit(solution)/shard_map/jit(_solve_triangular)/triangular_solve | solution.py:83
  562.8 2.8 copy.55
  572.5 6.8 fusion
  580.8 127.5 %all-reduce.10.cloned.1.call-done = (f32[512,512]{0,1:T(8,128)}, f32[512,256]{1,0:T(8,128)}) async-done(((f32[512,512]{0,1:T(8,128)}, f32[512,256]{1,0:T(8,128)}), (f32[512,512]{0,1:T(8,128)}, f32[512,256]{1,0:T(8,128)})) %all-reduce.10.cloned.1.call-update) | async-done | bytes 1572880 | tf_op jit(solution)/shard_map/psum | solution.py:11
  708.3 2.5 copy.59
  713.6 11.7 cholesky.358
  726.4 9.8 custom-call.35
  739.4 11.7 cholesky.377
  753.1 9.9 custom-call.36
  765.4 11.7 cholesky.398
  778.5 9.8 custom-call.37
  790.6 11.7 cholesky.415
  808.0 11.3 while.9
  808.7 2.2 bitcast_dynamic-update-slice_fusion.9
  811.5 2.2 bitcast_dynamic-update-slice_fusion.9
  814.4 2.2 bitcast_dynamic-update-slice_fusion.9
  817.2 2.1 bitcast_dynamic-update-slice_fusion.9
  819.3 39.9 %custom-call.38 = f32[4,128,128]{1,2,0:T(8,128)} custom-call(f32[4,128,128]{2,1,0:T(8,128)S(1)} %get-tuple-element.34), custom_call_target="InvertDiagBlocksLowerTriangular" | custom-call | tf_op jit(solution)/shard_map/jit(_solve_triangular)/triangular_solve | solution.py:52
  869.3 6.0 select_select_fusion
  875.3 4.1 copy.63
  879.4 57.6 %all_to_all.55 = f32[2,512,512]{2,0,1:T(2,128)S(1)} all-to-all(f32[2,512,512]{2,0,1:T(2,128)} %copy.63), channel_id=1, replica_groups=mesh['prow'=16,'pcol'=32] {'pcol'}, dimensions={1} | all-to-all | bytes 4194304 | tf_op jit(solution)/shard_map/all_to_all | solution.py:56
  939.5 43.1 %all-gather.3 = f32[1,512,256]{2,1,0:T(8,128)} all-gather(f32[1,16,256]{2,1,0:T(8,128)S(1)} %slice.178), channel_id=5, replica_groups=mesh['prow'=16,'pcol'=32] {'pcol'}, dimensions={1}, use_global_device_ids=true | all-gather | bytes 540672 | tf_op jit(solution)/shard_map/all_gather | solution.py:82
  982.5 32.6 %all-gather.15.cloned.1.call-done = f32[1,2,512,512]{3,1,0,2:T(2,128)} async-done(((f32[1,2,16,512]{3,1,0,2:T(2,128)}), f32[1,2,512,512]{3,1,0,2:T(2,128)}) %all-gather.15.cloned.1.call-update) | async-done | bytes 2097168 | tf_op jit(solution)/shard_map/all_gather | solution.py:60
  1015.1 4.0 fusion.153
  1020.3 11.8 all-to-all-start.3
  1032.2 7.4 while.11
  1040.4 40.1 %custom-call.40 = f32[4,128,128]{1,2,0:T(8,128)S(1)} custom-call(f32[4,128,128]{2,1,0:T(8,128)} %copy-done.11), custom_call_target="InvertDiagBlocksLowerTriangular" | custom-call | tf_op jit(solution)/shard_map/jit(_solve_triangular)/triangular_solve | solution.py:83
  1088.8 4.1 copy.66
  1093.8 105.9 %all-reduce.8.cloned.1.call-done = f32[512,256]{1,0:T(8,128)} async-done(((f32[512,256]{1,0:T(8,128)}), f32[512,256]{1,0:T(8,128)}) %all-reduce.8.cloned.1.call-update) | async-done | bytes 524304 | tf_op jit(solution)/shard_map/psum | solution.py:11
  1202.4 41.7 %all-gather.11.cloned.1.call-done = f32[512,512]{1,0:T(8,128)} async-done(((f32[32,512]{1,0:T(8,128)}), f32[512,512]{1,0:T(8,128)}) %all-gather.11.cloned.1.call-update) | async-done | bytes 1048592 | tf_op jit(solution)/shard_map/all_gather | solution.py:66
  1244.1 7.5 fusion.3
  1251.7 6.0 copy.72
  (188 shorter events, 100.8 us)
Async XLA Ops:
  7.2 1.2 slice-start
  7.2 126.8 %all-reduce.6.cloned.1.call-start = ((), (), s32[]{:S(2)}) async-start(), calls=%async_computation.4 | async-start | bytes 2097152 | tf_op jit(solution)/shard_map/psum | solution.py:11
  9.7 2.0 copy-start
  10.8 431.3 %all-gather.13.cloned.1.call-start = ((), (), s32[]{:S(2)}) async-start(), calls=%async_computation.8 | async-start | bytes 2162688 | tf_op jit(solution)/shard_map/all_gather | solution.py:60
  138.3 1.0 copy-start.5
  285.6 5.3 copy-start.10
  289.4 1.9 copy-start.2
  291.3 1.7 copy-start.6
  448.2 60.6 %all-to-all-start.1 = ((f32[16,32,512]{2,1,0:T(8,128)}), f32[16,32,512]{2,1,0:T(8,128)}, u32[]{:S(2)}, u32[]{:S(2)}) async-start(f32[16,32,512]{2,1,0:T(8,128)} %bitcast.227), calls=%async_computation.1 | async-start | bytes 2097152 | tf_op jit(solution)/shard_map/all_to_all | solution.py:64
  460.0 112.5 %all-gather.9.cloned.1.call-start = ((), (), s32[]{:S(2)}) async-start(), calls=%async_computation.5 | async-start | bytes 1114112 | tf_op jit(solution)/shard_map/all_gather | solution.py:66
  460.1 4.7 slice-start.1
  464.7 98.1 %copy-start.1 = (f32[1,2,512,512]{3,1,0,2:T(2,128)S(1)}, f32[1,2,512,512]{3,1,0,2:T(2,128)}, u32[]{:S(2)}) copy-start(f32[1,2,512,512]{3,1,0,2:T(2,128)} %all-gather.13.cloned.1.call-done) | copy-start | bytes 6291460
  510.3 198.0 %all-reduce.10.cloned.1.call-start = ((), (), s32[]{:S(2)}) async-start(), calls=%async_computation.10 | async-start | bytes 3145728 | tf_op jit(solution)/shard_map/psum | solution.py:11
  521.9 0.7 copy-start.12
  580.3 434.8 %all-gather.15.cloned.1.call-start = ((), (), s32[]{:S(2)}) async-start(), calls=%async_computation.9 | async-start | bytes 2162688 | tf_op jit(solution)/shard_map/all_gather | solution.py:60
  712.6 1.0 copy-start.4
  859.3 5.3 copy-start.9
  863.1 4.7 copy-start.3
  865.0 2.8 copy-start.7
  937.1 2.0 copy-start.8
  937.1 2.0 copy-start.13
  1020.3 66.9 %all-to-all-start.3 = ((f32[16,32,512]{2,1,0:T(8,128)}), f32[16,32,512]{2,1,0:T(8,128)}, u32[]{:S(2)}, u32[]{:S(2)}) async-start(f32[16,32,512]{2,1,0:T(8,128)} %bitcast.43), calls=%async_computation.3 | async-start | bytes 2097152 | tf_op jit(solution)/shard_map/all_to_all | solution.py:64
  1032.2 167.4 %all-reduce.8.cloned.1.call-start = ((), (), s32[]{:S(2)}) async-start(), calls=%async_computation.7 | async-start | bytes 1048576 | tf_op jit(solution)/shard_map/psum | solution.py:11
  1039.7 0.7 copy-start.11
  1087.2 156.9 %all-gather.11.cloned.1.call-start = ((), (), s32[]{:S(2)}) async-start(), calls=%async_computation.6 | async-start | bytes 1114112 | tf_op jit(solution)/shard_map/all_gather | solution.py:66
Sparse Core Ops, SparseCore 0:
  11.0 122.9 all-reduce.5
  365.6 76.4 all-gather.12
  510.4 51.0 all-gather.8
  580.5 127.7 all-reduce.9
  938.3 76.7 all-gather.14
  1087.3 112.2 all-reduce.7
  1202.0 42.0 all-gather.10
where the time goes:
time: 1280 us; the launch traced here: 1260 us
  waiting for transfers between devices  502 us (39%)
  other arithmetic  337 us (26%)
  blocking collectives  199 us (16%)
  local copies, waits for them, and re-layouts  108 us (8%)
  matrix products  73.9 us (6%)
  starting transfers between devices  24.3 us (2%)
  between operations  20.5 us (2%)
    psum x3, waiting for transfers between devices, broadcast(): return lax.psum(block, axis)  351 us
    another operation x29, other arithmetic, body(): diag_factor = jnp.linalg.cholesky(diagonal)  162 us
    all_to_all x2, blocking collectives, body(): lax.all_to_all(whole_panel, 'pcol', split_axis=1, concat_axis=0, tiled=True)  114 us
    all_gather x2, waiting for transfers between devices, body(): column_factor = lax.all_gather(own_share, 'pcol', axis=1, tiled=True)  109 us
    all_gather x2, blocking collectives, body(): gathered = lax.all_gather(pieces, 'pcol', axis=0, tiled=True)  84.7 us
    another operation x5, other arithmetic, body(): jax.scipy.linalg.solve_triangular(diag_factor, identity, lower=True)  84.5 us
    another operation x4, other arithmetic, body(): jax.scipy.linalg.solve_triangular(column_factor[local_row], gathered, low...  82.8 us
    all_gather x2, waiting for transfers between devices, body(): crossed.append(lax.all_gather(mine, 'prow', axis=0, tiled=True))  41.7 us
  transfers between devices with their start and end apart: 9, of which 6 were waited for; matrix products, arithmetic and copies ran while one was open for 11% of the time, Pallas kernels for 0%

commit v1 on v0

v1 whole, which is shorter than its diff:
```python
import functools

import jax
import jax.numpy as jnp
from jax import lax
from jax.experimental import pallas as pl
from jax.experimental.pallas import tpu as pltpu
from jax.sharding import PartitionSpec as P

HIGHEST = lax.Precision.HIGHEST
HIGH = lax.Precision.HIGH
MESH = pl.DeviceIdType.MESH
ROWS8 = 8
NY, NX, NZ = 8, 4, 8


def tn(a, b, precision=HIGH):
    return lax.dot_general(
        a, b, (((0,), (0,)), ((), ())), precision=precision, preferred_element_type=jnp.float32
    )


def nt(a, b, precision=HIGH):
    return lax.dot_general(
        a, b, (((1,), (1,)), ((), ())), precision=precision, preferred_element_type=jnp.float32
    )


def nn(a, b, precision=HIGH):
    return lax.dot_general(
        a, b, (((1,), (0,)), ((), ())), precision=precision, preferred_element_type=jnp.float32
    )


def lane_copy(x, i):
    return jnp.broadcast_to(x[:, i : i + 1], (8, 128))


def row_copy(ref, row):
    return ref[pl.ds(row, 8, stride=0), :]


def factor128(block, inv_ref, row_ref, col_ref, window=2, ahead=2, precision=HIGHEST):
    sub = lax.broadcasted_iota(jnp.int32, (8, 128), 0)
    lane = lax.broadcasted_iota(jnp.int32, (8, 128), 1)
    count = 16
    tiles = [block[8 * i : 8 * i + 8, :] for i in range(count)]
    group = []
    for t in range(count):
        g = t // window
        here = (lane >= 8 * t) & (lane < 8 * t + 8)
        row_ref[8 * t : 8 * t + 8, :] = tiles[t]
        rows = [
            jnp.where(here, jnp.where(lane == 8 * t + i, 1.0, 0.0), row_copy(row_ref, 8 * t + i))
            for i in range(8)
        ]
        base = 64 * (t % 2)
        for j in range(8):
            col_ref[base + 8 * j : base + 8 * j + 8, :] = lane_copy(tiles[t], 8 * t + j)
        s = {(i, k): row_copy(col_ref, base + 8 * i + k) for i in range(8) for k in range(i, 8)}
        later = list(range(t + 1, min((g + 1) * window + ahead, count)))
        cols = {q: [lane_copy(tiles[q], 8 * t + j) for j in range(8)] for q in later}
        rest = {q: jnp.where(here, 0.0, tiles[q]) for q in later}
        for j in range(8):
            r = lax.rsqrt(s[j, j])
            u = {k: s[j, k] * r for k in range(j + 1, 8)}
            for i in range(j + 1, 8):
                for k in range(i, 8):
                    s[i, k] = s[i, k] - u[i] * u[k]
            rows[j] = rows[j] * r
            for i in range(j + 1, 8):
                rows[i] = rows[i] - u[i] * rows[j]
            for q in later:
                m = cols[q][j] * r
                for k in range(j + 1, 8):
                    cols[q][k] = cols[q][k] - m * u[k]
                rest[q] = rest[q] - m * rows[j]
        done = rows[0]
        for i in range(1, 8):
            done = jnp.where(sub == i, rows[i], done)
        inv_ref[8 * t : 8 * t + 8, :] = jnp.where(lane < 8 * t + 8, done, 0.0)
        group.append(done)
        for q in later:
            tiles[q] = rest[q]
        if t % window == window - 1:
            first = (g + 1) * window + ahead
            if first < count:
                inside = (lane >= 8 * g * window) & (lane < 8 * (g + 1) * window)
                right = [
                    jnp.where(
                        (lane >= 8 * (g * window + a + 1)) & (lane < 8 * (g + 1) * window),
                        0.0,
                        group[a],
                    )
                    for a in range(window)
                ]
                v = tn(jnp.concatenate(group, 0), jnp.concatenate(right, 0), precision)
                for i in range(first, count):
                    tiles[i] = jnp.where(inside, 0.0, tiles[i]) - v[8 * i : 8 * i + 8, :]
            group = []


def compute_kernel(
    lead_ref, cross_ref, panel_ref, cov_ref, obs_ref, out_ref, red_ref,
    g, x, tile, mine, inv_a, inv_b, inv2, row_ref, col_ref, sems,
):
    p = lax.axis_index("prow")
    c = lax.axis_index("pcol")
    lead_in = pltpu.make_async_copy(lead_ref, g.at[:, 0:1280], sems.at[0])
    cross_in = pltpu.make_async_copy(cross_ref, g.at[:, 1280:1792], sems.at[1])
    panel_in = pltpu.make_async_copy(panel_ref, x, sems.at[2])
    tile_in = pltpu.make_async_copy(cov_ref, tile, sems.at[3])
    lead_in.start()
    cross_in.start()
    panel_in.start()
    tile_in.start()
    lead_in.wait()
    for big in range(4):
        lo, mid, hi = 256 * big, 256 * big + 128, 256 * big + 256
        factor128(g[lo:mid, lo:mid], inv_a, row_ref, col_ref)
        ia = inv_a[...]
        u = nn(ia, g[lo:mid, mid:hi], HIGHEST)
        factor128(g[mid:hi, mid:hi] - tn(u, u, HIGHEST), inv_b, row_ref, col_ref)
        ib = inv_b[...]
        inv2[0:128, 0:128] = ia
        inv2[0:128, 128:256] = jnp.zeros((128, 128), jnp.float32)
        inv2[128:256, 0:128] = -nn(ib, tn(u, ia, HIGHEST), HIGHEST)
        inv2[128:256, 128:256] = ib
        if big == 0:
            cross_in.wait()
            panel_in.wait()
        inv = inv2[...]
        for start in range(hi, 1792, 256):
            g[lo:hi, start : start + 256] = nn(inv, g[lo:hi, start : start + 256])
        for row in range(hi, 1024, 256):
            left = g[lo:hi, row : row + 256]
            for start in range(row, 1792, 256):
                g[row : row + 256, start : start + 256] -= tn(left, g[lo:hi, start : start + 256])

        @pl.loop(0, 4)
        def _(i):
            at = pl.ds(pl.multiple_of(i * 256, 256), 256)
            solved = nt(x[at, lo:hi], inv2[...])
            x[at, lo:hi] = solved
            for start in range(hi, 1024, 256):
                x[at, start : start + 256] -= nn(solved, g[lo:hi, start : start + 256])

    tile_in.wait()
    sub = lax.broadcasted_iota(jnp.int32, (256, 512), 0)
    lane = lax.broadcasted_iota(jnp.int32, (256, 512), 1)

    @pl.loop(0, 4)
    def _(i):
        at = pl.ds(pl.multiple_of(i * 256, 256), 256)
        below = p + 16 * (i // 2)

        @pl.when(c <= 1)
        def _():
            half = jnp.where(c == 0, x[at, 0:512], x[at, 512:1024])
            row = sub + 256 * (i % 2)
            keep = (below > c) | ((below == c) & (row >= lane))
            tile[at, :] = jnp.where(keep, half, 0.0)

        @pl.when((c > 1) & (below >= c))
        def _():
            tile[at, :] -= nn(x[at, :], g[:, 1280:1792])

        @pl.when((c > 1) & (below < c))
        def _():
            tile[at, :] = jnp.zeros((256, 512), jnp.float32)

    tile_out = pltpu.make_async_copy(tile, out_ref, sems.at[4])
    tile_out.start()
    y = g[:, 1024:1280]
    for r in range(2):
        at = pl.ds(pl.multiple_of(512 * r + 16 * c, 16), 16)
        strip = x[at, :]
        if r == 1:
            mine[...] = obs_ref[1] - nn(strip, y)
            red_ref[1] = mine[...]
        else:
            base = obs_ref[0]

            @pl.when(p > 1)
            def _():
                red_ref[0] = base - nn(strip, y)

            @pl.when(p <= 1)
            def _():
                rows = pl.ds(pl.multiple_of(512 * p + 16 * c, 16), 16)
                red_ref[0] = g[rows, 1024:1280]

    tile_out.wait()


def compute(lead, cross, panel, cov, obs):
    any_space = pl.BlockSpec(memory_space=pl.ANY)
    vmem = pl.BlockSpec(memory_space=pltpu.VMEM)
    return pl.pallas_call(
        compute_kernel,
        out_shape=[
            jax.ShapeDtypeStruct((1024, 512), jnp.float32),
            jax.ShapeDtypeStruct((2, 16, 256), jnp.float32),
        ],
        in_specs=[any_space, any_space, any_space, any_space, vmem],
        out_specs=[any_space, vmem],
        scratch_shapes=[
            pltpu.VMEM((1024, 1792), jnp.float32),
            pltpu.VMEM((1024, 1024), jnp.float32),
            pltpu.VMEM((1024, 512), jnp.float32),
            pltpu.VMEM((16, 256), jnp.float32),
            pltpu.VMEM((128, 128), jnp.float32),
            pltpu.VMEM((128, 128), jnp.float32),
            pltpu.VMEM((256, 256), jnp.float32),
            pltpu.VMEM((128, 128), jnp.float32),
            pltpu.VMEM((128, 128), jnp.float32),
            pltpu.SemaphoreType.DMA((5,)),
        ],
        compiler_params=pltpu.CompilerParams(vmem_limit_bytes=56 * 1024 * 1024),
    )(lead, cross, panel, cov, obs)


class Mover:
    def __init__(self, send_sems, recv_sems):
        self.send_sems, self.recv_sems, self.used, self.sent = send_sems, recv_sems, 0, []

    def copy(self, src, dst, device):
        slot = self.used
        self.used += 1
        return pltpu.make_async_remote_copy(
            src_ref=src, dst_ref=dst, send_sem=self.send_sems.at[slot],
            recv_sem=self.recv_sems.at[slot], device_id=device, device_id_type=MESH,
        )


def one_way(mover, view, size, me, step, device):
    half = 0 if step == 1 else 1
    for hop in range(1, size // 2 + 1):
        part = half if hop == size // 2 else None
        block = lax.rem(me - step * (hop - 1) + 2 * size, size)
        ref = view(block, part)
        copy = mover.copy(ref, ref, device)
        copy.start()
        mover.sent.append(copy)
        yield
        copy.wait_recv()


def both_ways(mover, view, size, me, ahead, behind):
    jobs = [one_way(mover, view, size, me, 1, ahead), one_way(mover, view, size, me, -1, behind)]
    while jobs:
        for job in list(jobs):
            try:
                next(job)
                yield
            except StopIteration:
                jobs.remove(job)


def move_kernel(cov_ref, obs_ref, panel, lead, cross, send_sems, recv_sems, wide_sems, local_sems):
    p = lax.axis_index("prow")
    c = lax.axis_index("pcol")
    z, core = p // 2, lax.rem(p, 2)
    y, x = c // NX, lax.rem(c, NX)

    def at(zz, yy, xx, cc=core):
        return (2 * zz + cc, yy * NX + xx)

    def ring(v, d, n):
        return lax.rem(v + d + n, n)

    xn, xp = at(z, y, ring(x, 1, NX)), at(z, y, ring(x, -1, NX))
    yn, yp = at(z, ring(y, 1, NY), x), at(z, ring(y, -1, NY), x)
    zn, zp = at(ring(z, 1, NZ), y, x), at(ring(z, -1, NZ), y, x)
    sibling = at(z, y, x, 1 - core)

    barrier = pltpu.get_barrier_semaphore()

    @pl.loop(1, 32)
    def _(d):
        pl.semaphore_signal(barrier, inc=1, device_id=(p, lax.rem(c + d, 32)), device_id_type=MESH)

    @pl.loop(1, 16)
    def _(d):
        pl.semaphore_signal(barrier, inc=1, device_id=(lax.rem(p + d, 16), c), device_id_type=MESH)

    pl.semaphore_wait(barrier, 46)

    mover = Mover(send_sems, recv_sems)

    def share(col, to):
        return (
            cov_ref.at[:, pl.ds(pl.multiple_of(to * 16, 16), 16), :],
            panel.at[:, to // NX, lax.rem(to, NX), :, 512 * col : 512 * col + 512],
        )

    def share_copy(col, to):
        src, dst = share(col, to)
        return pltpu.make_async_remote_copy(
            src_ref=src, dst_ref=dst, send_sem=wide_sems.at[0], recv_sem=wide_sems.at[1 + col],
            device_id=(p, to), device_id_type=MESH,
        )

    for col in range(2):

        @pl.when(c == col)
        def _():
            @pl.loop(1, 32)
            def _(d):
                share_copy(col, lax.rem(c + d, 32)).start()

            src, dst = share(col, c)
            own = pltpu.make_async_copy(src, dst, local_sems.at[0])
            own.start()
            own.wait()

    def slab(to):
        ref = cov_ref.at[0, pl.ds(pl.multiple_of(to * 64, 64), 64), :]
        return ref, cross.at[core, to]

    def slab_copy(to):
        src, dst = slab(to)
        return pltpu.make_async_remote_copy(
            src_ref=src, dst_ref=dst, send_sem=wide_sems.at[3], recv_sem=wide_sems.at[4],
            device_id=at(to, y, x), device_id_type=MESH,
        )

    def rhs_copy(to):
        return pltpu.make_async_remote_copy(
            src_ref=obs_ref.at[0], dst_ref=lead.at[core, y, x, :, 1024:1280],
            send_sem=wide_sems.at[5], recv_sem=wide_sems.at[6],
            device_id=at(to, y, x), device_id_type=MESH,
        )

    def lead_copy(to):
        return pltpu.make_async_remote_copy(
            src_ref=panel.at[0, y, x], dst_ref=lead.at[core, y, x, :, 0:1024],
            send_sem=wide_sems.at[7], recv_sem=wide_sems.at[8],
            device_id=at(to, y, x), device_id_type=MESH,
        )

    @pl.when(z == 0)
    def _():
        @pl.loop(1, NZ)
        def _(d):
            rhs_copy(d).start()
            slab_copy(d).start()

        src, dst = slab(0)
        own = pltpu.make_async_copy(src, dst, local_sems.at[1])
        own.start()
        own_rhs = pltpu.make_async_copy(
            obs_ref.at[0], lead.at[core, y, x, :, 1024:1280], local_sems.at[2]
        )
        own_rhs.start()
        own.wait()
        own_rhs.wait()

    for col in range(2):

        @pl.when(c != col)
        def _():
            share_copy(col, c).wait_recv()

    @pl.when(z == 0)
    def _():
        @pl.loop(1, NZ)
        def _(d):
            lead_copy(d).start()

        own = pltpu.make_async_copy(
            panel.at[0, y, x], lead.at[core, y, x, :, 0:1024], local_sems.at[3]
        )
        own.start()
        own.wait()

    def rows_of(ref, part, size):
        return ref if part is None else ref.at[pl.ds(part * size // 2, size // 2)]

    def y_then_x(where):
        def y_view(block, part):
            return rows_of(where(block, x), part, 16)

        def x_view(block, part):
            return where(slice(0, NY) if part is None else slice(4 * part, 4 * part + 4), block)

        yield from both_ways(mover, y_view, NY, y, yn, yp)
        yield from both_ways(mover, x_view, NX, x, xn, xp)

    def x_then_y(where):
        def x_view(block, part):
            return rows_of(where(y, block), part, 16)

        def y_view(block, part):
            return where(block, slice(0, NX) if part is None else slice(2 * part, 2 * part + 2))

        yield from both_ways(mover, x_view, NX, x, xn, xp)
        yield from both_ways(mover, y_view, NY, y, yn, yp)

    def lead_job():
        yield

        @pl.when(z != 0)
        def _():
            rhs_copy(0).wait_recv()
            lead_copy(0).wait_recv()

        yield from y_then_x(lambda yy, xx: lead.at[core, yy, xx])
        copy = mover.copy(lead.at[core], lead.at[core], sibling)
        copy.start()
        mover.sent.append(copy)
        yield
        copy.wait_recv()

    def cross_job():
        yield

        @pl.when(z != 0)
        def _():
            slab_copy(0).wait_recv()

        def view(block, part):
            return rows_of(cross.at[core, block], part, 64)

        yield from both_ways(mover, view, NZ, z, zn, zp)
        copy = mover.copy(cross.at[core], cross.at[core], sibling)
        copy.start()
        mover.sent.append(copy)
        yield
        copy.wait_recv()

    jobs = [
        x_then_y(lambda yy, xx: panel.at[1, yy, xx]),
        y_then_x(lambda yy, xx: panel.at[0, yy, xx]),
        cross_job(),
        lead_job(),
    ]
    while jobs:
        for job in list(jobs):
            try:
                next(job)
            except StopIteration:
                jobs.remove(job)
    for copy in mover.sent:
        copy.wait_send()

    for col in range(2):

        @pl.when(c == col)
        def _():
            @pl.loop(1, 32)
            def _(d):
                share_copy(col, lax.rem(c + d, 32)).wait_send()

    @pl.when(z == 0)
    def _():
        @pl.loop(1, NZ)
        def _(d):
            rhs_copy(d).wait_send()
            slab_copy(d).wait_send()
            lead_copy(d).wait_send()


def move(cov, obs):
    any_space = pl.BlockSpec(memory_space=pl.ANY)
    return pl.pallas_call(
        move_kernel,
        out_shape=[
            jax.ShapeDtypeStruct((2, NY, NX, 16, 1024), jnp.float32),
            jax.ShapeDtypeStruct((2, NY, NX, 16, 1280), jnp.float32),
            jax.ShapeDtypeStruct((2, NZ, 64, 512), jnp.float32),
        ],
        in_specs=[any_space] * 2,
        out_specs=[any_space] * 3,
        scratch_shapes=[
            pltpu.SemaphoreType.DMA((64,)),
            pltpu.SemaphoreType.DMA((64,)),
            pltpu.SemaphoreType.DMA((9,)),
            pltpu.SemaphoreType.DMA((4,)),
        ],
        compiler_params=pltpu.CompilerParams(collective_id=0, has_side_effects=True),
    )(cov, obs)


def body(covariance, observations):
    cov = covariance.reshape(2, 512, 512)
    obs = observations.reshape(2, 16, 256)
    panel, lead, cross = move(cov, obs)
    factor, reduced = compute(
        lead.reshape(1024, 1280), cross.reshape(1024, 512), panel.reshape(1024, 1024),
        cov.reshape(1024, 512), obs,
    )
    return factor.reshape(covariance.shape), reduced.reshape(observations.shape)


def solution(mesh):
    return jax.shard_map(
        body,
        mesh=mesh,
        in_specs=(P(None, "prow", None, None, "pcol", None), P(None, "prow", "pcol", None)),
        out_specs=(P(None, "prow", None, None, "pcol", None), P(None, "prow", "pcol", None)),
        check_vma=False,
    )
```

time: 1280 us -> 179 us (0.14)
  the two profiles are of different devices: /device:TPU:1 before, /device:TPU:16 now
where the time goes in v1:
time: 179 us; the launch traced here: 177 us
  Pallas kernels  168 us (94%)
  local copies, waits for them, and re-layouts  8.15 us (5%)
    pallas_call x1, Pallas kernels, move(): pl.pallas_call(move_kernel, out_shape=[jax.ShapeDtypeStruct((2, NY, NX, 1...  114 us
    pallas_call x1, Pallas kernels, compute(): pl.pallas_call(compute_kernel, out_shape=[jax.ShapeDtypeStruct((1024, 512...  54.8 us
    unnamed x2, local copies, waits for them, and re-layouts  8.15 us

profile of v1, /device:TPU:16, one launch (start us, length us, event | category | flops | bytes accessed | tf_op | source)
XLA Modules:
  0.0 177.2 jit_solution(16888975605498839772)
XLA Ops:
  0.6 3.1 %copy.10 = f32[2,1,512,1,1,512]{5,2,3,4,1,0:T(8,128)} copy(f32[2,1,512,1,1,512]{5,4,3,2,1,0:T(1,128)} %param.2) | data formatting | bytes 4194304
  3.7 113.6 %shard_map.41 = (f32[2,8,4,16,1024]{4,3,2,1,0:T(8,128)}, f32[2,8,4,16,1280]{4,3,2,1,0:T(8,128)}, f32[2,8,64,512]{3,2,1,0:T(8,128)}) custom-call(f32[2,512,512]{2,1,0:T(8,128)} %bitcast.11, f32[2,16,256]{2,1,0:T(8,128)} %bitcast.17), custom_call_target="tpu_custom_call" | custom-call | tf_op jit(solution)/shard_map/pallas_call | solution.py:466
  117.3 54.8 %shard_map.42 = (f32[1024,512]{1,0:T(8,128)}, f32[2,16,256]{2,1,0:T(8,128)}) custom-call(f32[1024,1280]{1,0:T(8,128)} %bitcast.13, f32[1024,512]{1,0:T(8,128)} %bitcast.16, f32[1024,1024]{1,0:T(8,128)} %bitcast.14, f32[1024,512]{1,0:T(8,128)} %bitcast.12, f32[2,16,256]{2,1,0:T(8,128)} %bitcast.18), custom_call_target="tpu_custom_call" | custom-call | tf_op jit(solution)/shard_map/pallas_call | solution.py:199
  172.2 5.1 %copy.4 = f32[2,1,512,1,1,512]{5,4,3,2,1,0:T(1,128)} copy(f32[2,1,512,1,1,512]{5,2,0,4,3,1:T(8,128)} %bitcast.15) | data formatting | bytes 4194304

commit v2 on v0

v2 whole, which is shorter than its diff:
```python
import functools

import jax
import jax.numpy as jnp
from jax import lax
from jax.experimental import pallas as pl
from jax.experimental.pallas import tpu as pltpu
from jax.sharding import PartitionSpec as P

HIGHEST = lax.Precision.HIGHEST
HIGH = lax.Precision.HIGH
MESH = pl.DeviceIdType.MESH
ROWS8 = 8
NY, NX, NZ = 8, 4, 8


def tn(a, b, precision=HIGH):
    return lax.dot_general(
        a, b, (((0,), (0,)), ((), ())), precision=precision, preferred_element_type=jnp.float32
    )


def nt(a, b, precision=HIGH):
    return lax.dot_general(
        a, b, (((1,), (1,)), ((), ())), precision=precision, preferred_element_type=jnp.float32
    )


def nn(a, b, precision=HIGH):
    return lax.dot_general(
        a, b, (((1,), (0,)), ((), ())), precision=precision, preferred_element_type=jnp.float32
    )


def lane_copy(x, i):
    return jnp.broadcast_to(x[:, i : i + 1], (8, 128))


def row_copy(ref, row):
    return ref[pl.ds(row, 8, stride=0), :]


def factor128(block, inv_ref, row_ref, col_ref, window=2, ahead=2, precision=HIGHEST):
    sub = lax.broadcasted_iota(jnp.int32, (8, 128), 0)
    lane = lax.broadcasted_iota(jnp.int32, (8, 128), 1)
    count = 16
    tiles = [block[8 * i : 8 * i + 8, :] for i in range(count)]
    group = []
    for t in range(count):
        g = t // window
        here = (lane >= 8 * t) & (lane < 8 * t + 8)
        row_ref[8 * t : 8 * t + 8, :] = tiles[t]
        rows = [
            jnp.where(here, jnp.where(lane == 8 * t + i, 1.0, 0.0), row_copy(row_ref, 8 * t + i))
            for i in range(8)
        ]
        base = 64 * (t % 2)
        for j in range(8):
            col_ref[base + 8 * j : base + 8 * j + 8, :] = lane_copy(tiles[t], 8 * t + j)
        s = {(i, k): row_copy(col_ref, base + 8 * i + k) for i in range(8) for k in range(i, 8)}
        later = list(range(t + 1, min((g + 1) * window + ahead, count)))
        cols = {q: [lane_copy(tiles[q], 8 * t + j) for j in range(8)] for q in later}
        rest = {q: jnp.where(here, 0.0, tiles[q]) for q in later}
        for j in range(8):
            r = lax.rsqrt(s[j, j])
            u = {k: s[j, k] * r for k in range(j + 1, 8)}
            for i in range(j + 1, 8):
                for k in range(i, 8):
                    s[i, k] = s[i, k] - u[i] * u[k]
            rows[j] = rows[j] * r
            for i in range(j + 1, 8):
                rows[i] = rows[i] - u[i] * rows[j]
            for q in later:
                m = cols[q][j] * r
                for k in range(j + 1, 8):
                    cols[q][k] = cols[q][k] - m * u[k]
                rest[q] = rest[q] - m * rows[j]
        done = rows[0]
        for i in range(1, 8):
            done = jnp.where(sub == i, rows[i], done)
        inv_ref[8 * t : 8 * t + 8, :] = jnp.where(lane < 8 * t + 8, done, 0.0)
        group.append(done)
        for q in later:
            tiles[q] = rest[q]
        if t % window == window - 1:
            first = (g + 1) * window + ahead
            if first < count:
                inside = (lane >= 8 * g * window) & (lane < 8 * (g + 1) * window)
                right = [
                    jnp.where(
                        (lane >= 8 * (g * window + a + 1)) & (lane < 8 * (g + 1) * window),
                        0.0,
                        group[a],
                    )
                    for a in range(window)
                ]
                v = tn(jnp.concatenate(group, 0), jnp.concatenate(right, 0), precision)
                for i in range(first, count):
                    tiles[i] = jnp.where(inside, 0.0, tiles[i]) - v[8 * i : 8 * i + 8, :]
            group = []


class Mover:
    def __init__(self, send_sems, recv_sems):
        self.send_sems, self.recv_sems, self.used, self.sent = send_sems, recv_sems, 0, []

    def copy(self, src, dst, device):
        slot = self.used
        self.used += 1

        def build():
            return pltpu.make_async_remote_copy(
                src_ref=src(), dst_ref=dst(), send_sem=self.send_sems.at[slot],
                recv_sem=self.recv_sems.at[slot], device_id=device, device_id_type=MESH,
            )

        return build


def all_to_all_peers(mover, views, size, me, device, active=None):
    copies = [
        mover.copy(functools.partial(view, me), functools.partial(view, me), device(lax.rem(me + d, size)))
        for view in views
        for d in range(1, size)
    ]

    def start():
        for copy in copies:
            copy().start()

    def wait():
        for copy in copies:
            copy().wait_recv()

    def end():
        for copy in copies:
            copy().wait_send()

    def guarded(f):
        if active is None:
            return f
        return lambda: pl.when(active)(f)

    mover.sent.append(guarded(end))
    return guarded(start), guarded(wait)


def ring(mover, view, size, me, device):
    steps = []
    for hop in range(1, size // 2 + 1):
        copies = []
        for side, step in ((0, 1), (1, -1)):
            part = side if hop == size // 2 else None
            block = lax.rem(me - step * (hop - 1) + 2 * size, size)
            ref = functools.partial(view, block, part)
            copies.append(mover.copy(ref, ref, device(lax.rem(me + step + size, size))))

        def start(copies=copies):
            for copy in copies:
                copy().start()

        def wait(copies=copies):
            for copy in copies:
                copy().wait_recv()

        def end(copies=copies):
            for copy in copies:
                copy().wait_send()

        mover.sent.append(end)
        steps.append((start, wait))
    return steps


def move_kernel(
    cov_ref, obs_ref, panel, rhs, cross, upper, inverses,
    lead, work, row_ref, col_ref, send_sems, recv_sems, wide_sems, local_sems,
):
    p = lax.axis_index("prow")
    c = lax.axis_index("pcol")
    z, core = p // 2, lax.rem(p, 2)
    y, x = c // NX, lax.rem(c, NX)

    def at(zz, yy, xx, cc=core):
        return (2 * zz + cc, yy * NX + xx)

    def x_device(v):
        return at(z, y, v)

    def y_device(v):
        return at(z, v, x)

    def z_device(v):
        return at(v, y, x)

    sibling = at(z, y, x, 1 - core)

    barrier = pltpu.get_barrier_semaphore()

    def greet(device):
        pl.semaphore_signal(barrier, inc=1, device_id=device, device_id_type=MESH)

    for d in range(1, NY):
        greet(y_device(lax.rem(y + d, NY)))
    for d in range(1, NX):
        greet(x_device(lax.rem(x + d, NX)))
    for d in range(1, NZ):
        greet(z_device(lax.rem(z + d, NZ)))
    greet(sibling)
    for col in range(2):

        @pl.when(c == col)
        def _():
            @pl.loop(1, 32)
            def _(d):
                greet((p, lax.rem(c + d, 32)))

        @pl.when(c != col)
        def _():
            greet((p, col))

    others = NY + NX + NZ - 2
    pl.semaphore_wait(
        barrier,
        others + jnp.where(c != 0, 1, 0) + jnp.where(c != 1, 1, 0) + jnp.where(c <= 1, 31, 0),
    )

    mover = Mover(send_sems, recv_sems)

    def remote(src, dst, send, recv, device):
        return pltpu.make_async_remote_copy(
            src_ref=src, dst_ref=dst, send_sem=wide_sems.at[send], recv_sem=wide_sems.at[recv],
            device_id=device, device_id_type=MESH,
        )

    def local(src, dst, slot):
        return pltpu.make_async_copy(src, dst, local_sems.at[slot])

    def rows16(ref, to):
        return ref.at[pl.ds(pl.multiple_of(to * 16, 16), 16), :]

    def lead_share(half, to):
        dst = lead.at[core, to // NX, lax.rem(to, NX), :, 512 * half : 512 * half + 512]
        return remote(rows16(cov_ref.at[0], to), dst, 2 * half, 2 * half + 1, (p, to))

    def lead_sender(half):
        return (c == half) & ((p == 0) if half == 0 else (z == 0))

    def lead_plane(half):
        return (p == 0) if half == 0 else (z == 0)

    def start_lead(half):
        @pl.when(lead_sender(half))
        def _():
            @pl.loop(1, 32)
            def _(d):
                lead_share(half, lax.rem(c + d, 32)).start()

            own = local(
                rows16(cov_ref.at[0], c), lead.at[core, y, x, :, 512 * half : 512 * half + 512], half
            )
            own.start()
            own.wait()

    def end_lead(half):
        @pl.when(lead_sender(half))
        def _():
            @pl.loop(1, 32)
            def _(d):
                lead_share(half, lax.rem(c + d, 32)).wait_send()

    def wait_lead(half):
        @pl.when(lead_plane(half) & (c != half))
        def _():
            lead_share(half, c).wait_recv()

    def lead_down(half, to):
        ref = lead.at[core, y, x, :, 512 * half : 512 * half + 512]
        return remote(ref, ref, 4 + 2 * half, 5 + 2 * half, z_device(to))

    def on_lead(half, condition):
        return (condition & (core == 0)) if half == 0 else condition

    def start_down(half):
        @pl.when(on_lead(half, z == 0))
        def _():
            @pl.loop(1, NZ)
            def _(d):
                lead_down(half, d).start()

    def wait_down(half):
        @pl.when(on_lead(half, z != 0))
        def _():
            lead_down(half, 0).wait_recv()

    def end_down(half):
        @pl.when(on_lead(half, z == 0))
        def _():
            @pl.loop(1, NZ)
            def _(d):
                lead_down(half, d).wait_send()

    def share(col, to):
        return (
            cov_ref.at[:, pl.ds(pl.multiple_of(to * 16, 16), 16), :],
            panel.at[:, to // NX, lax.rem(to, NX), :, 512 * col : 512 * col + 512],
        )

    def share_copy(col, to):
        src, dst = share(col, to)
        return remote(src, dst, 8, 9 + col, (p, to))

    def slab_copy(to):
        src = cov_ref.at[0, pl.ds(pl.multiple_of(to * 64, 64), 64), :]
        return remote(src, cross.at[core, to], 11, 12, z_device(to))

    def rhs_copy(to):
        return remote(obs_ref.at[0], rhs.at[core, y, x], 13, 14, z_device(to))

    start_lead(0)
    start_lead(1)

    @pl.when(z == 0)
    def _():
        @pl.loop(1, NZ)
        def _(d):
            rhs_copy(d).start()

        own = local(obs_ref.at[0], rhs.at[core, y, x], 2)
        own.start()
        own.wait()

    end_lead(0)
    end_lead(1)
    for col in range(2):

        @pl.when(c == col)
        def _():
            @pl.loop(1, 32)
            def _(d):
                share_copy(col, lax.rem(c + d, 32)).start()

            src, dst = share(col, c)
            own = local(src, dst, 3)
            own.start()
            own.wait()

    def lead_y(half):
        return lambda block: lead.at[core, block, x, :, 512 * half : 512 * half + 512]

    def lead_x(half):
        return lambda block: lead.at[core, :, block, :, 512 * half : 512 * half + 512]

    def rhs_y(block):
        return rhs.at[core, block, x]

    def rhs_x(block):
        return rhs.at[core, :, block]

    def peers(views, size, me, device, active=None):
        return all_to_all_peers(mover, views, size, me, device, active)

    first_slots = mover.used
    mover.used += NY

    def first_y(d):
        ref = lead_y(0)(y)
        return pltpu.make_async_remote_copy(
            src_ref=ref, dst_ref=ref, send_sem=send_sems.at[first_slots + d],
            recv_sem=recv_sems.at[first_slots + y], device_id=y_device(lax.rem(y + d, NY)),
            device_id_type=MESH,
        )

    def first_y_wait(v):
        ref = lead_y(0)(v)
        return pltpu.make_async_remote_copy(
            src_ref=ref, dst_ref=ref, send_sem=send_sems.at[first_slots],
            recv_sem=recv_sems.at[first_slots + v], device_id=y_device(v), device_id_type=MESH,
        )

    def pair_rows(q, block):
        return lead.at[0, 2 * q : 2 * q + 2, block, :, 0:512]

    first_x = [
        [
            mover.copy(
                functools.partial(pair_rows, q, x), functools.partial(pair_rows, q, x),
                x_device(lax.rem(x + d, NX)),
            )
            for d in range(1, NX)
        ]
        for q in range(4)
    ]
    first_pair = [
        mover.copy(
            functools.partial(pair_rows, q, slice(0, NX)),
            functools.partial(pair_rows, q, slice(0, NX)), sibling,
        )
        for q in range(4)
    ]

    def y_arrived(q):
        @pl.when(core == 0)
        def _():
            for v in (2 * q, 2 * q + 1):

                @pl.when(y != v)
                def _():
                    first_y_wait(v).wait_recv()

            for copy in first_x[q]:
                copy().start()

    def x_arrived(q):
        @pl.when(core == 0)
        def _():
            for copy in first_x[q]:
                copy().wait_recv()
            first_pair[q]().start()

    def pair_arrived(q):
        @pl.when(core == 1)
        def _():
            first_pair[q]().wait_recv()

    def whole_or_half(view):
        return lambda block, part: view(
            slice(0, NY) if part is None else slice(4 * part, 4 * part + 4), block
        )

    second_y = peers([lead_y(1), rhs_y], NY, y, y_device)
    second_x = ring(
        mover, whole_or_half(lambda rows, block: lead.at[core, rows, block, :, 512:1024]),
        NX, x, x_device,
    )
    rhs_ring = ring(
        mover, whole_or_half(lambda rows, block: rhs.at[core, rows, block]), NX, x, x_device
    )
    cross_z = peers([lambda block: cross.at[core, block]], NZ, z, z_device)
    low_y = peers([lambda block: panel.at[0, block, x]], NY, y, y_device)
    high_x = peers([lambda block: panel.at[1, y, block]], NX, x, x_device)
    low_x = ring(
        mover,
        lambda block, part: panel.at[
            0, slice(0, NY) if part is None else slice(4 * part, 4 * part + 4), block
        ],
        NX, x, x_device,
    )
    high_y = ring(
        mover,
        lambda block, part: panel.at[
            1, block, slice(0, NX) if part is None else slice(2 * part, 2 * part + 2)
        ],
        NY, y, y_device,
    )

    def to_sibling(view):
        build = mover.copy(view, view, sibling)
        mover.sent.append(lambda: build().wait_send())
        return lambda: build().start(), lambda: build().wait_recv()

    second_pair = to_sibling(lambda: lead.at[core, :, :, :, 512:1024])
    rhs_pair = to_sibling(lambda: rhs.at[core])
    cross_pair = to_sibling(lambda: cross.at[core])

    wait_lead(0)
    start_down(0)
    wait_lead(1)
    start_down(1)
    wait_down(0)

    @pl.when(core == 0)
    def _():
        for d in range(1, NY):
            first_y(d).start()

    @pl.when(z == 0)
    def _():
        @pl.loop(1, NZ)
        def _(d):
            slab_copy(d).start()

        own = local(cov_ref.at[0, 0:64, :], cross.at[core, 0], 4)
        own.start()
        own.wait()

    y_arrived(0)
    y_arrived(1)

    @pl.when(z != 0)
    def _():
        rhs_copy(0).wait_recv()

    wait_down(1)
    second_y[0]()
    y_arrived(2)
    y_arrived(3)
    x_arrived(0)
    x_arrived(1)
    for col in range(2):

        @pl.when(c != col)
        def _():
            share_copy(col, c).wait_recv()

    high_x[0]()
    low_y[0]()
    second_y[1]()
    second_x[0][0]()
    rhs_ring[0][0]()

    @pl.when(z != 0)
    def _():
        slab_copy(0).wait_recv()

    cross_z[0]()
    pair_arrived(0)

    def slot0():
        x_arrived(2)
        pair_arrived(1)
        high_x[1]()
        high_y[0][0]()
        second_x[0][1]()
        rhs_ring[0][1]()
        second_x[1][0]()
        rhs_ring[1][0]()

    def slot1():
        x_arrived(3)
        pair_arrived(2)
        low_y[1]()
        low_x[0][0]()
        second_x[1][1]()
        second_pair[0]()
        rhs_ring[1][1]()
        rhs_pair[0]()
        high_y[0][1]()
        high_y[1][0]()

    def slot2():
        pair_arrived(3)
        high_y[1][1]()
        high_y[2][0]()
        low_x[0][1]()
        low_x[1][0]()

    def slot3():
        second_pair[1]()

    def slot4():
        high_y[2][1]()
        high_y[3][0]()
        cross_z[1]()
        cross_pair[0]()

    def slot6():
        rhs_pair[1]()
        low_x[1][1]()
        high_y[3][1]()
        cross_pair[1]()

    slots = {0: slot0, 1: slot1, 2: slot2, 3: slot3, 4: slot4, 6: slot6}

    upper[...] = jnp.zeros((1024, 1024), jnp.float32)

    @pl.loop(0, 8)
    def _(a):
        at_row = pl.ds(pl.multiple_of(128 * lax.rem(a, 4), 128), 128)
        at_wide = pl.ds(pl.multiple_of(512 * (a // 4), 512), 512)
        at_upper = pl.ds(pl.multiple_of(128 * a, 128), 128)

        @pl.when(a < 4)
        def _():
            for i in range(8):
                work[pl.ds(pl.multiple_of(128 * a + 16 * i, 16), 16), :] = lead[
                    0, 2 * a + i // NX, i % NX, :, 0:512
                ]

        @pl.when(a == 4)
        def _():
            for i in range(32):
                upper[16 * i : 16 * i + 16, 512:1024] = lead[0, i // NX, i % NX, :, 512:1024]
                work[16 * i : 16 * i + 16, :] = lead[1, i // NX, i % NX, :, 512:1024]
            for k in range(4):
                rows = slice(128 * k, 128 * k + 128)
                if k:
                    upper[rows, 512:1024] -= tn(
                        upper[0 : 128 * k, rows], upper[0 : 128 * k, 512:1024], HIGHEST
                    )
                upper[rows, 512:1024] = nn(inverses[k], upper[rows, 512:1024], HIGHEST)

            @pl.loop(0, 4)
            def _(i):
                cut = pl.ds(pl.multiple_of(128 * i, 128), 128)
                left = upper[0:512, pl.ds(pl.multiple_of(512 + 128 * i, 128), 128)]
                work[cut, :] -= tn(left, upper[0:512, 512:1024], HIGHEST)

        work[at_row, :] -= tn(upper[at_wide, at_upper], upper[at_wide, at_wide], HIGHEST)
        factor128(work[at_row, at_row], inverses.at[a], row_ref, col_ref)
        upper[at_upper, at_wide] = nn(inverses[a], work[at_row, :], HIGHEST)
        for index, events in slots.items():
            pl.when(a == index)(events)

    for end in mover.sent:
        end()

    @pl.when(core == 0)
    def _():
        for d in range(1, NY):
            first_y(d).wait_send()
        for q in range(4):
            for copy in first_x[q]:
                copy().wait_send()
            first_pair[q]().wait_send()

    end_down(0)
    end_down(1)
    for col in range(2):

        @pl.when(c == col)
        def _():
            @pl.loop(1, 32)
            def _(d):
                share_copy(col, lax.rem(c + d, 32)).wait_send()

    @pl.when(z == 0)
    def _():
        @pl.loop(1, NZ)
        def _(d):
            rhs_copy(d).wait_send()
            slab_copy(d).wait_send()


def move(cov, obs):
    any_space = pl.BlockSpec(memory_space=pl.ANY)
    vmem = pl.BlockSpec(memory_space=pltpu.VMEM)
    return pl.pallas_call(
        move_kernel,
        out_shape=[
            jax.ShapeDtypeStruct((2, NY, NX, 16, 1024), jnp.float32),
            jax.ShapeDtypeStruct((2, NY, NX, 16, 256), jnp.float32),
            jax.ShapeDtypeStruct((2, NZ, 64, 512), jnp.float32),
            jax.ShapeDtypeStruct((1024, 1024), jnp.float32),
            jax.ShapeDtypeStruct((8, 128, 128), jnp.float32),
        ],
        in_specs=[any_space] * 2,
        out_specs=[any_space] * 3 + [vmem] * 2,
        scratch_shapes=[
            pltpu.VMEM((2, NY, NX, 16, 1024), jnp.float32),
            pltpu.VMEM((512, 512), jnp.float32),
            pltpu.VMEM((128, 128), jnp.float32),
            pltpu.VMEM((128, 128), jnp.float32),
            pltpu.SemaphoreType.DMA((96,)),
            pltpu.SemaphoreType.DMA((96,)),
            pltpu.SemaphoreType.DMA((15,)),
            pltpu.SemaphoreType.DMA((5,)),
        ],
        compiler_params=pltpu.CompilerParams(
            collective_id=0, has_side_effects=True, vmem_limit_bytes=60 * 1024 * 1024
        ),
    )(cov, obs)


def update_kernel(
    upper_ref, inverses_ref, rhs_ref, cross_ref, panel_ref, cov_ref, obs_ref, out_ref, red_ref,
    u, inv, g, x, tile, flat, inv2, sems,
):
    p = lax.axis_index("prow")
    c = lax.axis_index("pcol")
    loads = [
        pltpu.make_async_copy(inverses_ref, inv, sems.at[0]),
        pltpu.make_async_copy(upper_ref, u, sems.at[1]),
        pltpu.make_async_copy(rhs_ref, g.at[:, 512:768], sems.at[2]),
        pltpu.make_async_copy(cross_ref, g.at[:, 0:512], sems.at[3]),
        pltpu.make_async_copy(panel_ref, x, sems.at[4]),
        pltpu.make_async_copy(cov_ref, tile, sems.at[5]),
    ]
    for load in loads:
        load.start()
    for load in loads[:2]:
        load.wait()
    for big in range(4):
        lo, mid, hi = 256 * big, 256 * big + 128, 256 * big + 256
        ia, ib = inv[2 * big], inv[2 * big + 1]
        inv2[big, 0:128, 0:128] = ia
        inv2[big, 0:128, 128:256] = jnp.zeros((128, 128), jnp.float32)
        inv2[big, 128:256, 0:128] = -nn(ib, tn(u[lo:mid, mid:hi], ia, HIGHEST), HIGHEST)
        inv2[big, 128:256, 128:256] = ib
    for load in loads[2:5]:
        load.wait()
    for big in range(4):
        lo, hi = 256 * big, 256 * big + 256
        g[lo:hi, :] = nn(inv2[big], g[lo:hi, :])
        for row in range(hi, 1024, 256):
            g[row : row + 256, :] -= tn(u[lo:hi, row : row + 256], g[lo:hi, :])

        @pl.loop(0, 4)
        def _(i):
            at = pl.ds(pl.multiple_of(i * 256, 256), 256)
            solved = nt(x[at, lo:hi], inv2[big])
            x[at, lo:hi] = solved
            for start in range(hi, 1024, 256):
                x[at, start : start + 256] -= nn(solved, u[lo:hi, start : start + 256])

    loads[5].wait()
    sub = lax.broadcasted_iota(jnp.int32, (256, 512), 0)
    lane = lax.broadcasted_iota(jnp.int32, (256, 512), 1)

    def put(i, values):
        for row in range(32):
            for col in range(4):
                flat[pl.ds(1024 * i + 32 * row + col, 8, stride=4), :] = values[
                    8 * row : 8 * row + 8, 128 * col : 128 * col + 128
                ]

    for i in range(4):
        at = pl.ds(256 * i, 256)
        below = p + 16 * (i // 2)

        @pl.when(c <= 1)
        def _():
            half = jnp.where(c == 0, x[at, 0:512], x[at, 512:1024])
            row = sub + 256 * (i % 2)
            keep = (below > c) | ((below == c) & (row >= lane))
            put(i, jnp.where(keep, half, 0.0))

        @pl.when((c > 1) & (below >= c))
        def _():
            put(i, tile[at, :] - nn(x[at, :], g[:, 0:512]))

        @pl.when((c > 1) & (below < c))
        def _():
            flat[pl.ds(1024 * i, 1024), :] = jnp.zeros((1024, 128), jnp.float32)

    tile_out = pltpu.make_async_copy(flat, out_ref, sems.at[6])
    tile_out.start()
    solved_rhs = g[:, 512:768]
    low = x[pl.ds(pl.multiple_of(16 * c, 16), 16), :]
    high = x[pl.ds(pl.multiple_of(512 + 16 * c, 16), 16), :]
    red_ref[1] = obs_ref[1] - nn(high, solved_rhs)

    @pl.when(p > 1)
    def _():
        red_ref[0] = obs_ref[0] - nn(low, solved_rhs)

    @pl.when(p <= 1)
    def _():
        red_ref[0] = g[pl.ds(pl.multiple_of(512 * p + 16 * c, 16), 16), 512:768]

    tile_out.wait()


def update(upper, inverses, rhs, cross, panel, cov, obs):
    any_space = pl.BlockSpec(memory_space=pl.ANY)
    vmem = pl.BlockSpec(memory_space=pltpu.VMEM)
    return pl.pallas_call(
        update_kernel,
        out_shape=[
            jax.ShapeDtypeStruct((4096, 128), jnp.float32),
            jax.ShapeDtypeStruct((2, 16, 256), jnp.float32),
        ],
        in_specs=[any_space] * 6 + [vmem],
        out_specs=[any_space, vmem],
        scratch_shapes=[
            pltpu.VMEM((1024, 1024), jnp.float32),
            pltpu.VMEM((8, 128, 128), jnp.float32),
            pltpu.VMEM((1024, 768), jnp.float32),
            pltpu.VMEM((1024, 1024), jnp.float32),
            pltpu.VMEM((1024, 512), jnp.float32),
            pltpu.VMEM((4096, 128), jnp.float32),
            pltpu.VMEM((4, 256, 256), jnp.float32),
            pltpu.SemaphoreType.DMA((7,)),
        ],
        compiler_params=pltpu.CompilerParams(vmem_limit_bytes=60 * 1024 * 1024),
    )(upper, inverses, rhs, cross, panel, cov, obs)


def body(covariance, observations):
    cov = covariance.reshape(2, 512, 512)
    obs = observations.reshape(2, 16, 256)
    panel, rhs, cross, upper, inverses = move(cov, obs)
    factor, reduced = update(
        upper, inverses, rhs.reshape(1024, 256), cross.reshape(1024, 512),
        panel.reshape(1024, 1024), cov.reshape(1024, 512), obs,
    )
    return factor.reshape(covariance.shape), reduced.reshape(observations.shape)


def solution(mesh):
    return jax.shard_map(
        body,
        mesh=mesh,
        in_specs=(P(None, "prow", None, None, "pcol", None), P(None, "prow", "pcol", None)),
        out_specs=(P(None, "prow", None, None, "pcol", None), P(None, "prow", "pcol", None)),
        check_vma=False,
    )
```

time: 1280 us -> 155 us (0.12)
  the two profiles are of different devices: /device:TPU:1 before, /device:TPU:24 now
where the time goes in v2:
time: 155 us; the launch traced here: 154 us
  Pallas kernels  150 us (97%)
  local copies, waits for them, and re-layouts  3.14 us (2%)
    pallas_call x1, Pallas kernels, move(): pl.pallas_call(move_kernel, out_shape=[jax.ShapeDtypeStruct((2, NY, NX, 1...  126 us
    pallas_call x1, Pallas kernels, update(): pl.pallas_call(update_kernel, out_shape=[jax.ShapeDtypeStruct((4096, 128)...  24.4 us
    unnamed x1, local copies, waits for them, and re-layouts  3.14 us

profile of v2, /device:TPU:24, one launch (start us, length us, event | category | flops | bytes accessed | tf_op | source)
XLA Modules:
  0.0 154.3 jit_solution(5922013106217654751)
XLA Ops:
  0.6 3.1 %copy.10 = f32[2,1,512,1,1,512]{5,2,3,4,1,0:T(8,128)} copy(f32[2,1,512,1,1,512]{5,4,3,2,1,0:T(1,128)} %param.2) | data formatting | bytes 4194304
  3.8 126.0 %shard_map.41 = (f32[2,8,4,16,1024]{4,3,2,1,0:T(8,128)}, f32[2,8,4,16,256]{4,3,2,1,0:T(8,128)}, f32[2,8,64,512]{3,2,1,0:T(8,128)}, f32[1024,1024]{1,0:T(8,128)}, f32[8,128,128]{2,1,0:T(8,128)}) custom-call(f32[2,512,512]{2,1,0:T(8,128)} %bitcast.11, f32[2,16,256]{2,1,0:T(8,128)} %bitcast.16), custom_call_target="tpu_custom_call" | custom-call | tf_op jit(solution)/shard_map/pallas_call | solution.py:638
  129.7 24.4 %shard_map.42 = (f32[4096,128]{1,0:T(8,128)}, f32[2,16,256]{2,1,0:T(8,128)}) custom-call(f32[1024,1024]{1,0:T(8,128)} %get-tuple-element.9.upper_ref, f32[8,128,128]{2,1,0:T(8,128)} %get-tuple-element.10.inverses_ref, f32[1024,256]{1,0:T(8,128)} %bitcast.15, f32[1024,512]{1,0:T(8,128)} %bitcast.14, f32[1024,1024]{1,0:T(8,128)} %bitcast.13, ...), custom_call_target="tpu_custom_call" | custom-call | tf_op jit(solution)/shard_map/pallas_call | solution.py:757

commit v3 on v2

--- a/solution.py
+++ b/solution.py
@@ -145,7 +145,7 @@
     return guarded(start), guarded(wait)
 
 
-def ring(mover, view, size, me, device):
+def ring(mover, view, size, me, device, active=None):
     steps = []
     for hop in range(1, size // 2 + 1):
         copies = []
@@ -167,6 +167,10 @@
             for copy in copies:
                 copy().wait_send()
 
+        if active is not None:
+            start, wait, end = (
+                functools.partial(lambda f: pl.when(active)(f), f) for f in (start, wait, end)
+            )
         mover.sent.append(end)
         steps.append((start, wait))
     return steps
@@ -174,7 +178,7 @@
 
 def move_kernel(
     cov_ref, obs_ref, panel, rhs, cross, upper, inverses,
-    lead, work, row_ref, col_ref, send_sems, recv_sems, wide_sems, local_sems,
+    lead, stage, work, row_ref, col_ref, send_sems, recv_sems, wide_sems, local_sems,
 ):
     p = lax.axis_index("prow")
     c = lax.axis_index("pcol")
@@ -236,18 +240,33 @@
     def local(src, dst, slot):
         return pltpu.make_async_copy(src, dst, local_sems.at[slot])
 
-    def rows16(ref, to):
-        return ref.at[pl.ds(pl.multiple_of(to * 16, 16), 16), :]
+    def rows16(row, to):
+        return cov_ref.at[row, to // NX, lax.rem(to, NX)]
+
+    def lead_home(half, to):
+        return stage if half else lead.at[core, to // NX, lax.rem(to, NX), :, 0:512]
+
+    def piece(ref, part):
+        rows = pl.ds(pl.multiple_of(8 * (part // 4), 8), 8)
+        return ref.at[rows, pl.ds(pl.multiple_of(128 * lax.rem(part, 4), 128), 128)]
+
+    def second(part, ys, xs):
+        rows = pl.ds(pl.multiple_of(8 * (part // 4), 8), 8)
+        lanes = pl.ds(pl.multiple_of(512 + 128 * lax.rem(part, 4), 128), 128)
+        return lead.at[core, ys, xs, rows, lanes]
 
     def lead_share(half, to):
-        dst = lead.at[core, to // NX, lax.rem(to, NX), :, 512 * half : 512 * half + 512]
-        return remote(rows16(cov_ref.at[0], to), dst, 2 * half, 2 * half + 1, (p, to))
+        dst = lead_home(half, to)
+        return remote(rows16(0, to), dst, 2 * half, 2 * half + 1, (p, to))
 
     def lead_sender(half):
         return (c == half) & ((p == 0) if half == 0 else (z == 0))
 
     def lead_plane(half):
         return (p == 0) if half == 0 else (z == 0)
+
+    def own_lead(half):
+        return local(rows16(0, c), lead_home(half, c), half)
 
     def start_lead(half):
         @pl.when(lead_sender(half))
@@ -256,11 +275,7 @@
             def _(d):
                 lead_share(half, lax.rem(c + d, 32)).start()
 
-            own = local(
-                rows16(cov_ref.at[0], c), lead.at[core, y, x, :, 512 * half : 512 * half + 512], half
-            )
-            own.start()
-            own.wait()
+            own_lead(half).start()
 
     def end_lead(half):
         @pl.when(lead_sender(half))
@@ -274,9 +289,18 @@
         def _():
             lead_share(half, c).wait_recv()
 
+        @pl.when(lead_sender(half))
+        def _():
+            own_lead(half).wait()
+
     def lead_down(half, to):
-        ref = lead.at[core, y, x, :, 512 * half : 512 * half + 512]
-        return remote(ref, ref, 4 + 2 * half, 5 + 2 * half, z_device(to))
+        if half:
+            return remote(piece(stage, to), second(to, y, x), 6, 7, z_device(to))
+        ref = lead_home(0, c)
+        return remote(ref, ref, 4, 5, z_device(to))
+
+    def own_piece():
+        return local(stage.at[0:8, 0:128], lead.at[core, y, x, 0:8, 512:640], 6)
 
     def on_lead(half, condition):
         return (condition & (core == 0)) if half == 0 else condition
@@ -288,6 +312,10 @@
             def _(d):
                 lead_down(half, d).start()
 
+            if half:
+                own_piece().start()
+                own_piece().wait()
+
     def wait_down(half):
         @pl.when(on_lead(half, z != 0))
         def _():
@@ -300,56 +328,68 @@
             def _(d):
                 lead_down(half, d).wait_send()
 
-    def share(col, to):
-        return (
-            cov_ref.at[:, pl.ds(pl.multiple_of(to * 16, 16), 16), :],
-            panel.at[:, to // NX, lax.rem(to, NX), :, 512 * col : 512 * col + 512],
-        )
-
     def share_copy(col, to):
-        src, dst = share(col, to)
-        return remote(src, dst, 8, 9 + col, (p, to))
+        dst = panel.at[0, to // NX, lax.rem(to, NX), :, 512 * col : 512 * col + 512]
+        return remote(rows16(0, to), dst, 8, 9 + col, (p, to))
+
+    def high_part(col, to):
+        return panel.at[1, to, :, :, 512 * col : 512 * col + 512]
+
+    def high_share(col, to):
+        return remote(cov_ref.at[1, to], high_part(col, to), 15, 16 + col, y_device(to))
+
+    def high_cast(col, to):
+        return remote(high_part(col, y), high_part(col, y), 18, 19 + col, x_device(to))
 
     def slab_copy(to):
-        src = cov_ref.at[0, pl.ds(pl.multiple_of(to * 64, 64), 64), :]
-        return remote(src, cross.at[core, to], 11, 12, z_device(to))
+        return remote(cov_ref.at[0, to], cross.at[core, to], 11, 12, z_device(to))
 
     def rhs_copy(to):
         return remote(obs_ref.at[0], rhs.at[core, y, x], 13, 14, z_device(to))
 
+    def own_high(col):
+        return local(cov_ref.at[1, 0], high_part(col, 0), 5)
+
+    def own_low(col):
+        return local(rows16(0, c), panel.at[0, y, x, :, 512 * col : 512 * col + 512], 3)
+
+    def own_rhs():
+        return local(obs_ref.at[0], rhs.at[core, y, x], 2)
+
+    def own_slab():
+        return local(cov_ref.at[0, 0], cross.at[core, 0], 4)
+
+    def both_columns(condition, action):
+        for col in range(2):
+            pl.when(condition(col))(functools.partial(action, col))
+
     start_lead(0)
     start_lead(1)
 
+    def start_high(col):
+        for d in range(1, NY):
+            high_share(col, d).start()
+        own_high(col).start()
+
+    both_columns(lambda col: c == col, start_high)
+
     @pl.when(z == 0)
     def _():
-        @pl.loop(1, NZ)
+        for d in range(1, NZ):
+            rhs_copy(d).start()
+        own_rhs().start()
+
+    def start_low(col):
+        @pl.loop(1, 32)
         def _(d):
-            rhs_copy(d).start()
-
-        own = local(obs_ref.at[0], rhs.at[core, y, x], 2)
-        own.start()
-        own.wait()
-
-    end_lead(0)
-    end_lead(1)
-    for col in range(2):
-
-        @pl.when(c == col)
-        def _():
-            @pl.loop(1, 32)
-            def _(d):
-                share_copy(col, lax.rem(c + d, 32)).start()
-
-            src, dst = share(col, c)
-            own = local(src, dst, 3)
-            own.start()
-            own.wait()
+            share_copy(col, lax.rem(c + d, 32)).start()
+
+        own_low(col).start()
+
+    both_columns(lambda col: (c == col) & (z != 0), start_low)
 
     def lead_y(half):
         return lambda block: lead.at[core, block, x, :, 512 * half : 512 * half + 512]
-
-    def lead_x(half):
-        return lambda block: lead.at[core, :, block, :, 512 * half : 512 * half + 512]
 
     def rhs_y(block):
         return rhs.at[core, block, x]
@@ -428,23 +468,50 @@
             slice(0, NY) if part is None else slice(4 * part, 4 * part + 4), block
         )
 
-    second_y = peers([lead_y(1), rhs_y], NY, y, y_device)
-    second_x = ring(
-        mover, whole_or_half(lambda rows, block: lead.at[core, rows, block, :, 512:1024]),
-        NX, x, x_device,
+    second_y = peers([lambda block: second(z, block, x)], NY, y, y_device)
+    second_x = peers([lambda block: second(z, slice(0, NY), block)], NX, x, x_device)
+    second_z = ring(
+        mover,
+        lambda block, part: second(
+            block, slice(0, NY) if part is None else slice(4 * part, 4 * part + 4), slice(0, NX)
+        ),
+        NZ, z, z_device,
     )
+    rhs_gather = peers([rhs_y], NY, y, y_device)
     rhs_ring = ring(
         mover, whole_or_half(lambda rows, block: rhs.at[core, rows, block]), NX, x, x_device
     )
     cross_z = peers([lambda block: cross.at[core, block]], NZ, z, z_device)
-    low_y = peers([lambda block: panel.at[0, block, x]], NY, y, y_device)
-    high_x = peers([lambda block: panel.at[1, y, block]], NX, x, x_device)
+    low_rows = z // 2
+    low_copies = [
+        mover.copy(
+            lambda: panel.at[0, y, x], lambda: panel.at[0, y, x], y_device(lax.rem(y + d, NY))
+        )
+        for d in range(1, NY)
+    ]
+
+    def low_y_start():
+        for d, copy in enumerate(low_copies, 1):
+            pl.when(lax.rem(y + d, NY) <= low_rows)(lambda copy=copy: copy().start())
+
+    def low_y_end():
+        for d, copy in enumerate(low_copies, 1):
+            pl.when(lax.rem(y + d, NY) <= low_rows)(lambda copy=copy: copy().wait_send())
+
+    mover.sent.append(low_y_end)
+
+    def low_y_wait():
+        @pl.when(y <= low_rows)
+        def _():
+            for copy in low_copies:
+                copy().wait_recv()
+
     low_x = ring(
         mover,
         lambda block, part: panel.at[
             0, slice(0, NY) if part is None else slice(4 * part, 4 * part + 4), block
         ],
-        NX, x, x_device,
+        NX, x, x_device, y <= low_rows,
     )
     high_y = ring(
         mover,
@@ -467,6 +534,39 @@
     start_down(0)
     wait_lead(1)
     start_down(1)
+    both_columns(lambda col: (c == col) & (z == 0), start_low)
+
+    @pl.when(z == 0)
+    def _():
+        for d in range(1, NZ):
+            slab_copy(d).start()
+        own_slab().start()
+
+    def cast_high(col):
+        @pl.when(y != 0)
+        def _():
+            high_share(col, y).wait_recv()
+
+        @pl.when(y == 0)
+        def _():
+            own_high(col).wait()
+
+        for d in range(1, NX):
+            high_cast(col, lax.rem(x + d, NX)).start()
+
+    def high_arrived():
+        for col in range(2):
+
+            @pl.when(x != col)
+            def _():
+                high_cast(col, col).wait_recv()
+
+    def low_arrived(where):
+        both_columns(lambda col: (c != col) & where, lambda col: share_copy(col, c).wait_recv())
+        both_columns(lambda col: (c == col) & where, lambda col: own_low(col).wait())
+        pl.when(where)(low_y_start)
+
+    both_columns(lambda col: x == col, cast_high)
     wait_down(0)
 
     @pl.when(core == 0)
@@ -474,93 +574,88 @@
         for d in range(1, NY):
             first_y(d).start()
 
-    @pl.when(z == 0)
-    def _():
-        @pl.loop(1, NZ)
-        def _(d):
-            slab_copy(d).start()
-
-        own = local(cov_ref.at[0, 0:64, :], cross.at[core, 0], 4)
-        own.start()
-        own.wait()
-
+    wait_down(1)
+    second_y[0]()
+    low_arrived(z != 0)
     y_arrived(0)
     y_arrived(1)
+    second_y[1]()
+    second_x[0]()
+    y_arrived(2)
+    y_arrived(3)
+    second_x[1]()
+    second_z[0][0]()
+    high_arrived()
+    high_y[0][0]()
+    x_arrived(0)
+    x_arrived(1)
+    second_z[0][1]()
+    second_z[1][0]()
 
     @pl.when(z != 0)
     def _():
         rhs_copy(0).wait_recv()
-
-    wait_down(1)
-    second_y[0]()
-    y_arrived(2)
-    y_arrived(3)
-    x_arrived(0)
-    x_arrived(1)
-    for col in range(2):
-
-        @pl.when(c != col)
-        def _():
-            share_copy(col, c).wait_recv()
-
-    high_x[0]()
-    low_y[0]()
-    second_y[1]()
-    second_x[0][0]()
-    rhs_ring[0][0]()
-
-    @pl.when(z != 0)
+        slab_copy(0).wait_recv()
+
+    @pl.when(z == 0)
     def _():
-        slab_copy(0).wait_recv()
-
-    cross_z[0]()
+        own_rhs().wait()
+        own_slab().wait()
+
+    low_arrived(z == 0)
+    rhs_gather[0]()
     pair_arrived(0)
 
     def slot0():
         x_arrived(2)
         pair_arrived(1)
-        high_x[1]()
-        high_y[0][0]()
-        second_x[0][1]()
-        rhs_ring[0][1]()
-        second_x[1][0]()
-        rhs_ring[1][0]()
+        second_z[1][1]()
+        second_z[2][0]()
+        high_y[0][1]()
+        high_y[1][0]()
+        low_y_wait()
+        low_x[0][0]()
 
     def slot1():
         x_arrived(3)
         pair_arrived(2)
-        low_y[1]()
-        low_x[0][0]()
-        second_x[1][1]()
+        second_z[2][1]()
+        second_z[3][0]()
+        rhs_gather[1]()
+        rhs_ring[0][0]()
+        high_y[1][1]()
+        high_y[2][0]()
+
+    def slot2():
+        pair_arrived(3)
+        second_z[3][1]()
         second_pair[0]()
+        cross_z[0]()
+        rhs_ring[0][1]()
+        rhs_ring[1][0]()
+        low_x[0][1]()
+        low_x[1][0]()
+        high_y[2][1]()
+        high_y[3][0]()
+
+    def slot3():
+        second_pair[1]()
+
+    def slot4():
         rhs_ring[1][1]()
         rhs_pair[0]()
-        high_y[0][1]()
-        high_y[1][0]()
-
-    def slot2():
-        pair_arrived(3)
-        high_y[1][1]()
-        high_y[2][0]()
-        low_x[0][1]()
-        low_x[1][0]()
-
-    def slot3():
-        second_pair[1]()
-
-    def slot4():
-        high_y[2][1]()
-        high_y[3][0]()
+        high_y[3][1]()
+        low_x[1][1]()
+
+    def slot6():
         cross_z[1]()
         cross_pair[0]()
 
-    def slot6():
+    def slot7():
         rhs_pair[1]()
-        low_x[1][1]()
-        high_y[3][1]()
         cross_pair[1]()
 
-    slots = {0: slot0, 1: slot1, 2: slot2, 3: slot3, 4: slot4, 6: slot6}
+    slots = {0: slot0, 1: slot1, 2: slot2, 3: slot3, 4: slot4, 6: slot6, 7: slot7}
 
     upper[...] = jnp.zeros((1024, 1024), jnp.float32)
 
@@ -614,6 +709,8 @@
                 copy().wait_send()
             first_pair[q]().wait_send()
 
+    end_lead(0)
+    end_lead(1)
     end_down(0)
     end_down(1)
     for col in range(2):
@@ -623,6 +720,15 @@
             @pl.loop(1, 32)
             def _(d):
                 share_copy(col, lax.rem(c + d, 32)).wait_send()
+
+            @pl.loop(1, NY)
+            def _(d):
+                high_share(col, d).wait_send()
+
+        @pl.when(x == col)
+        def _():
+            for d in range(1, NX):
+                high_cast(col, lax.rem(x + d, NX)).wait_send()
 
     @pl.when(z == 0)
     def _():
@@ -640,7 +746,7 @@
         out_shape=[
             jax.ShapeDtypeStruct((2, NY, NX, 16, 1024), jnp.float32),
             jax.ShapeDtypeStruct((2, NY, NX, 16, 256), jnp.float32),
-            jax.ShapeDtypeStruct((2, NZ, 64, 512), jnp.float32),
+            jax.ShapeDtypeStruct((2, NZ, 4, 16, 512), jnp.float32),
             jax.ShapeDtypeStruct((1024, 1024), jnp.float32),
             jax.ShapeDtypeStruct((8, 128, 128), jnp.float32),
         ],
@@ -648,13 +754,14 @@
         out_specs=[any_space] * 3 + [vmem] * 2,
         scratch_shapes=[
             pltpu.VMEM((2, NY, NX, 16, 1024), jnp.float32),
+            pltpu.VMEM((16, 512), jnp.float32),
             pltpu.VMEM((512, 512), jnp.float32),
             pltpu.VMEM((128, 128), jnp.float32),
             pltpu.VMEM((128, 128), jnp.float32),
             pltpu.SemaphoreType.DMA((96,)),
             pltpu.SemaphoreType.DMA((96,)),
-            pltpu.SemaphoreType.DMA((15,)),
-            pltpu.SemaphoreType.DMA((5,)),
+            pltpu.SemaphoreType.DMA((21,)),
+            pltpu.SemaphoreType.DMA((7,)),
         ],
         compiler_params=pltpu.CompilerParams(
             collective_id=0, has_side_effects=True, vmem_limit_bytes=60 * 1024 * 1024
@@ -779,7 +886,7 @@
 def body(covariance, observations):
     cov = covariance.reshape(2, 512, 512)
     obs = observations.reshape(2, 16, 256)
-    panel, rhs, cross, upper, inverses = move(cov, obs)
+    panel, rhs, cross, upper, inverses = move(cov.reshape(2, NY, NX, 16, 512), obs)
     factor, reduced = update(
         upper, inverses, rhs.reshape(1024, 256), cross.reshape(1024, 512),
         panel.reshape(1024, 1024), cov.reshape(1024, 512), obs,

time: 155 us -> 145 us (0.935)
  the two profiles are of different devices: /device:TPU:24 before, /device:TPU:16 now
where the time goes in v3:
time: 145 us
  Pallas kernels  141 us (97%)
  local copies, waits for them, and re-layouts  3.14 us (2%)
    pallas_call x1, Pallas kernels, move(): pl.pallas_call(move_kernel, out_shape=[jax.ShapeDtypeStruct((2, NY, NX, 1...  117 us
    pallas_call x1, Pallas kernels, update(): pl.pallas_call(update_kernel, out_shape=[jax.ShapeDtypeStruct((4096, 128)...  24.4 us
    unnamed x1, local copies, waits for them, and re-layouts  3.14 us

profile of v3, /device:TPU:16, one launch (start us, length us, event | category | flops | bytes accessed | tf_op | source)
XLA Modules:
  0.0 144.9 jit_solution(17044846987129808303)
XLA Ops:
  0.6 3.1 %copy.6 = f32[2,1,512,1,1,512]{5,2,3,4,1,0:T(8,128)} copy(f32[2,1,512,1,1,512]{5,4,3,2,1,0:T(1,128)} %param.2) | data formatting | bytes 4194304
  3.8 116.6 %shard_map.41 = (f32[2,8,4,16,1024]{4,3,2,1,0:T(8,128)}, f32[2,8,4,16,256]{4,3,2,1,0:T(8,128)}, f32[2,8,4,16,512]{4,3,2,1,0:T(8,128)}, f32[1024,1024]{1,0:T(8,128)}, f32[8,128,128]{2,1,0:T(8,128)}) custom-call(f32[2,8,4,16,512]{4,3,2,1,0:T(8,128)} %bitcast.10, f32[2,16,256]{2,1,0:T(8,128)} %bitcast.15), custom_call_target="tpu_custom_call" | custom-call | tf_op jit(solution)/shard_map/pallas_call | solution.py:744
  120.4 24.4 %shard_map.42 = (f32[4096,128]{1,0:T(8,128)}, f32[2,16,256]{2,1,0:T(8,128)}) custom-call(f32[1024,1024]{1,0:T(8,128)} %get-tuple-element.9.upper_ref, f32[8,128,128]{2,1,0:T(8,128)} %get-tuple-element.10.inverses_ref, f32[1024,256]{1,0:T(8,128)} %bitcast.14, f32[1024,512]{1,0:T(8,128)} %bitcast.13, f32[1024,1024]{1,0:T(8,128)} %bitcast.12, ...), custom_call_target="tpu_custom_call" | custom-call | tf_op jit(solution)/shard_map/pallas_call | solution.py:864

commit v4 on v3

--- a/solution.py
+++ b/solution.py
@@ -386,8 +386,6 @@
 
         own_low(col).start()
 
-    both_columns(lambda col: (c == col) & (z != 0), start_low)
-
     def lead_y(half):
         return lambda block: lead.at[core, block, x, :, 512 * half : 512 * half + 512]
 
@@ -481,7 +479,13 @@
     rhs_ring = ring(
         mover, whole_or_half(lambda rows, block: rhs.at[core, rows, block]), NX, x, x_device
     )
-    cross_z = peers([lambda block: cross.at[core, block]], NZ, z, z_device)
+    cross_z = ring(
+        mover,
+        lambda block, part: (
+            cross.at[core, block] if part is None else cross.at[core, block, 2 * part : 2 * part + 2]
+        ),
+        NZ, z, z_device,
+    )
     low_rows = z // 2
     low_copies = [
         mover.copy(
@@ -534,8 +538,6 @@
     start_down(0)
     wait_lead(1)
     start_down(1)
-    both_columns(lambda col: (c == col) & (z == 0), start_low)
-
     @pl.when(z == 0)
     def _():
         for d in range(1, NZ):
@@ -561,12 +563,11 @@
             def _():
                 high_cast(col, col).wait_recv()
 
-    def low_arrived(where):
-        both_columns(lambda col: (c != col) & where, lambda col: share_copy(col, c).wait_recv())
-        both_columns(lambda col: (c == col) & where, lambda col: own_low(col).wait())
-        pl.when(where)(low_y_start)
-
-    both_columns(lambda col: x == col, cast_high)
+    def low_arrived():
+        both_columns(lambda col: c != col, lambda col: share_copy(col, c).wait_recv())
+        both_columns(lambda col: c == col, lambda col: own_low(col).wait())
+        low_y_start()
+
     wait_down(0)
 
     @pl.when(core == 0)
@@ -576,19 +577,18 @@
 
     wait_down(1)
     second_y[0]()
-    low_arrived(z != 0)
     y_arrived(0)
     y_arrived(1)
     second_y[1]()
     second_x[0]()
     y_arrived(2)
     y_arrived(3)
+    both_columns(lambda col: c == col, start_low)
     second_x[1]()
     second_z[0][0]()
-    high_arrived()
-    high_y[0][0]()
     x_arrived(0)
     x_arrived(1)
+    both_columns(lambda col: x == col, cast_high)
     second_z[0][1]()
     second_z[1][0]()
 
@@ -602,7 +602,7 @@
         own_rhs().wait()
         own_slab().wait()
 
-    low_arrived(z == 0)
+    cross_z[0][0]()
     rhs_gather[0]()
     pair_arrived(0)
 
@@ -611,51 +611,59 @@
         pair_arrived(1)
         second_z[1][1]()
         second_z[2][0]()
-        high_y[0][1]()
-        high_y[1][0]()
-        low_y_wait()
-        low_x[0][0]()
+        cross_z[0][1]()
+        cross_z[1][0]()
+        low_arrived()
 
     def slot1():
         x_arrived(3)
         pair_arrived(2)
         second_z[2][1]()
         second_z[3][0]()
-        rhs_gather[1]()
-        rhs_ring[0][0]()
-        high_y[1][1]()
-        high_y[2][0]()
+        high_arrived()
+        high_y[0][0]()
+        cross_z[1][1]()
+        cross_z[2][0]()
 
     def slot2():
         pair_arrived(3)
         second_z[3][1]()
         second_pair[0]()
-        cross_z[0]()
+        high_y[0][1]()
+        high_y[1][0]()
+        low_y_wait()
+        low_x[0][0]()
+        cross_z[2][1]()
+        cross_z[3][0]()
+        rhs_gather[1]()
+
+    def slot3():
+        second_pair[1]()
+        high_y[1][1]()
+        high_y[2][0]()
+        cross_z[3][1]()
+        cross_pair[0]()
+        rhs_ring[0][0]()
+
+    def slot4():
+        high_y[2][1]()
+        high_y[3][0]()
+        low_x[0][1]()
+        low_x[1][0]()
         rhs_ring[0][1]()
         rhs_ring[1][0]()
-        low_x[0][1]()
-        low_x[1][0]()
-        high_y[2][1]()
-        high_y[3][0]()
-
-    def slot3():
-        second_pair[1]()
-
-    def slot4():
+
+    def slot5():
         rhs_ring[1][1]()
         rhs_pair[0]()
+
+    def slot6():
         high_y[3][1]()
         low_x[1][1]()
-
-    def slot6():
-        cross_z[1]()
-        cross_pair[0]()
-
-    def slot7():
         rhs_pair[1]()
         cross_pair[1]()
 
-    slots = {0: slot0, 1: slot1, 2: slot2, 3: slot3, 4: slot4, 6: slot6, 7: slot7}
+    slots = {0: slot0, 1: slot1, 2: slot2, 3: slot3, 4: slot4, 5: slot5, 6: slot6}
 
     upper[...] = jnp.zeros((1024, 1024), jnp.float32)
 
@@ -802,9 +810,8 @@
         for row in range(hi, 1024, 256):
             g[row : row + 256, :] -= tn(u[lo:hi, row : row + 256], g[lo:hi, :])
 
-        @pl.loop(0, 4)
-        def _(i):
-            at = pl.ds(pl.multiple_of(i * 256, 256), 256)
+        for i in range(4):
+            at = slice(256 * i, 256 * i + 256)
             solved = nt(x[at, lo:hi], inv2[big])
             x[at, lo:hi] = solved
             for start in range(hi, 1024, 256):

time: 145 us -> 131 us (0.903)
  Pallas kernels: 141 us -> 126 us
    pallas_call x1, Pallas kernels: 117 us -> 108 us  [move(): pl.pallas_call(move_kernel, out_shape=[jax.ShapeDtypeStruct((2, NY, NX, 1...]
    pallas_call x1, Pallas kernels: 24.4 us -> 18.5 us  [update(): pl.pallas_call(update_kernel, out_shape=[jax.ShapeDtypeStruct((4096, 128)...]
where the time goes in v4:
time: 131 us; the launch traced here: 130 us
  Pallas kernels  126 us (96%)
  local copies, waits for them, and re-layouts  3.14 us (2%)
    pallas_call x1, Pallas kernels, move(): pl.pallas_call(move_kernel, out_shape=[jax.ShapeDtypeStruct((2, NY, NX, 1...  108 us
    pallas_call x1, Pallas kernels, update(): pl.pallas_call(update_kernel, out_shape=[jax.ShapeDtypeStruct((4096, 128)...  18.5 us
    unnamed x1, local copies, waits for them, and re-layouts  3.14 us

profile of v4, /device:TPU:16, one launch (start us, length us, event | category | flops | bytes accessed | tf_op | source)
XLA Modules:
  0.0 130.4 jit_solution(16353889707991096625)
XLA Ops:
  0.6 3.1 %copy.6 = f32[2,1,512,1,1,512]{5,2,3,4,1,0:T(8,128)} copy(f32[2,1,512,1,1,512]{5,4,3,2,1,0:T(1,128)} %param.2) | data formatting | bytes 4194304
  3.8 107.9 %shard_map.41 = (f32[2,8,4,16,1024]{4,3,2,1,0:T(8,128)}, f32[2,8,4,16,256]{4,3,2,1,0:T(8,128)}, f32[2,8,4,16,512]{4,3,2,1,0:T(8,128)}, f32[1024,1024]{1,0:T(8,128)}, f32[8,128,128]{2,1,0:T(8,128)}) custom-call(f32[2,8,4,16,512]{4,3,2,1,0:T(8,128)} %bitcast.10, f32[2,16,256]{2,1,0:T(8,128)} %bitcast.15), custom_call_target="tpu_custom_call" | custom-call | tf_op jit(solution)/shard_map/pallas_call | solution.py:752
  111.7 18.5 %shard_map.42 = (f32[4096,128]{1,0:T(8,128)}, f32[2,16,256]{2,1,0:T(8,128)}) custom-call(f32[1024,1024]{1,0:T(8,128)} %get-tuple-element.9.upper_ref, f32[8,128,128]{2,1,0:T(8,128)} %get-tuple-element.10.inverses_ref, f32[1024,256]{1,0:T(8,128)} %bitcast.14, f32[1024,512]{1,0:T(8,128)} %bitcast.13, f32[1024,1024]{1,0:T(8,128)} %bitcast.12, ...), custom_call_target="tpu_custom_call" | custom-call | tf_op jit(solution)/shard_map/pallas_call | solution.py:871

commit v5 on v4

--- a/solution.py
+++ b/solution.py
@@ -371,8 +371,6 @@
             high_share(col, d).start()
         own_high(col).start()
 
-    both_columns(lambda col: c == col, start_high)
-
     @pl.when(z == 0)
     def _():
         for d in range(1, NZ):
@@ -574,6 +572,8 @@
     def _():
         for d in range(1, NY):
             first_y(d).start()
+
+    both_columns(lambda col: c == col, start_high)
 
     wait_down(1)
     second_y[0]()

time: 131 us -> 128 us (0.977)
  the two profiles are of different devices: /device:TPU:16 before, /device:TPU:68 now
where the time goes in v5:
time: 128 us
  Pallas kernels  124 us (97%)
  local copies, waits for them, and re-layouts  3.14 us (2%)
    pallas_call x1, Pallas kernels, move(): pl.pallas_call(move_kernel, out_shape=[jax.ShapeDtypeStruct((2, NY, NX, 1...  104 us
    pallas_call x1, Pallas kernels, update(): pl.pallas_call(update_kernel, out_shape=[jax.ShapeDtypeStruct((4096, 128)...  20.5 us
    unnamed x1, local copies, waits for them, and re-layouts  3.14 us

profile of v5, /device:TPU:68, one launch (start us, length us, event | category | flops | bytes accessed | tf_op | source)
XLA Modules:
  0.0 128.0 jit_solution(10774824045857418775)
XLA Ops:
  0.6 3.1 %copy.6 = f32[2,1,512,1,1,512]{5,2,3,4,1,0:T(8,128)} copy(f32[2,1,512,1,1,512]{5,4,3,2,1,0:T(1,128)} %param.2) | data formatting | bytes 4194304
  3.8 103.5 %shard_map.41 = (f32[2,8,4,16,1024]{4,3,2,1,0:T(8,128)}, f32[2,8,4,16,256]{4,3,2,1,0:T(8,128)}, f32[2,8,4,16,512]{4,3,2,1,0:T(8,128)}, f32[1024,1024]{1,0:T(8,128)}, f32[8,128,128]{2,1,0:T(8,128)}) custom-call(f32[2,8,4,16,512]{4,3,2,1,0:T(8,128)} %bitcast.10, f32[2,16,256]{2,1,0:T(8,128)} %bitcast.15), custom_call_target="tpu_custom_call" | custom-call | tf_op jit(solution)/shard_map/pallas_call | solution.py:752
  107.3 20.5 %shard_map.42 = (f32[4096,128]{1,0:T(8,128)}, f32[2,16,256]{2,1,0:T(8,128)}) custom-call(f32[1024,1024]{1,0:T(8,128)} %get-tuple-element.9.upper_ref, f32[8,128,128]{2,1,0:T(8,128)} %get-tuple-element.10.inverses_ref, f32[1024,256]{1,0:T(8,128)} %bitcast.14, f32[1024,512]{1,0:T(8,128)} %bitcast.13, f32[1024,1024]{1,0:T(8,128)} %bitcast.12, ...), custom_call_target="tpu_custom_call" | custom-call | tf_op jit(solution)/shard_map/pallas_call | solution.py:871
